TPU v7x, 256 devices: a whole 4x4x8 slice. The times are simulated.
256 devices in a mesh: tm: 32 (over x_hi, z, core), space: 8 (over y, x_lo).
Axes of the slice: x: 4 (x_hi: 2, x_lo: 2; x = x_hi * 2 + x_lo), y: 4, z: 8, core: 2. Of those that a mesh axis runs over, the one named last changes fastest.
Arguments:
- queries: bfloat16 [32768, 1536], P(('tm', 'space')), may hold values from -24 to 24
- keys: bfloat16 [32768, 1536], P(('tm', 'space')), may hold values from -24 to 24
- values: bfloat16 [32768, 1536], P(('tm', 'space')), may hold values from -8 to 8
- tile_mask: int32 [32, 32], replicated, may hold values from 0 to 1, as said below
- inner_x: bfloat16 [32768, 1536], P(('tm', 'space')), may hold values from -140 to 140
- bc_proj: bfloat16 [32768, 128], P(('tm', 'space')), may hold values from -4 to 4
- log_decay: bfloat16 [24, 32768], P(None, ('tm', 'space')), may hold values from -1 to 0
- col_order: int32 [32], replicated, may hold values from 0 to 31, each once
- norm_gain: float32 [1536], replicated, may hold values from 0.1 to 1.9
Outputs:
- mixed: bfloat16 [32768, 1536], P(('tm', 'space'))
Inputs may be any that keep to these rules, and one draw needn't show every extreme that they name: `tile_mask`: 1 on the diagonal and for frames exactly 8 before or after around the loop; 0 for frames more than 8 away around the loop.
All inputs are finite; a program needn't handle non-finite values.
Results may differ from a plain program's by a relative error of at most 0.017.
Values may be sent and summed in bfloat16 or wider, within the bound.
No kernel may reach another device: no remote copies, remote signals or barrier semaphores. Data moves between devices by JAX's collectives and lax.ppermute only.
A program may use at most 384 MiB of HBM per device.

v0:
```python
import jax
import jax.numpy as jnp
from jax import lax
from jax.sharding import PartitionSpec as P

HEADS = 12
HEAD_DIM = 128
SCAN_HEADS = 24
SCAN_DIM = 64
STATE_DIM = 64
ROWS_DEV = 4
COLS = 32


EPS = 1e-05
FLOOR = -1e30


def carried_in(array, axis, join, neutral):
    place = lax.axis_index(axis)
    gathered = jax.tree.map(
        lambda a, kind: lax.all_gather(a.astype(kind), axis), array, (jnp.bfloat16, jnp.bfloat16)
    )
    state = jax.tree.map(lambda a, e: jnp.zeros_like(a) + jnp.asarray(e, a.dtype), array, neutral)

    def carried_one(lap, state):
        return join(
            state,
            jax.tree.map(
                lambda a, own: lax.dynamic_index_in_dim(a, lap, 0, False).astype(own.dtype),
                gathered,
                array,
            ),
        )

    return lax.fori_loop(0, place, carried_one, state)


def for_sending(array):

    def short(part):
        return part.astype(jnp.bfloat16) if part.dtype == jnp.float32 else part

    return jax.tree.map(short, array)


def from_root(array, axis, root):
    mine = lax.axis_index(axis) == root
    return lax.psum(jnp.where(mine, array, jnp.zeros_like(array)), axis)


def prefix(array, axis, join, neutral):
    place = lax.axis_index(axis)
    gathered = jax.tree.map(
        lambda a, kind: lax.all_gather(a.astype(kind), axis),
        array,
        jax.tree.map(lambda a: jnp.bfloat16 if a.dtype == jnp.float32 else a.dtype, array),
    )
    state = jax.tree.map(lambda a, e: jnp.zeros_like(a) + jnp.asarray(e, a.dtype), array, neutral)

    def prefix_one(lap, state):
        return join(
            state,
            jax.tree.map(
                lambda a, own: lax.dynamic_index_in_dim(a, lap, 0, False).astype(own.dtype),
                gathered,
                array,
            ),
        )

    return lax.fori_loop(0, place, prefix_one, state)


def shifted(array, axis, by):
    devices = lax.axis_size(axis)
    return lax.ppermute(array, axis, [(i, (i + by) % devices) for i in range(devices)])


def absorb(flash_state, query_rows, key_rows, value_rows, allowed, score_scale):
    running_max, totals, accum = flash_state
    row_count = key_rows.shape[0]
    key_rows = key_rows.reshape(row_count, HEADS, HEAD_DIM)
    value_rows = value_rows.reshape(row_count, HEADS, HEAD_DIM)
    scores = (
        jnp.einsum("qhd,khd->hqk", query_rows, key_rows, preferred_element_type=jnp.float32)
        * score_scale
    )
    scores = jnp.where(allowed[None, None, :], scores, FLOOR)
    new_max = jnp.maximum(running_max, jnp.max(scores, axis=2))
    weights = jnp.where(allowed[None, None, :], jnp.exp(scores - new_max[:, :, None]), 0.0)
    factor = jnp.exp(running_max - new_max)
    totals = totals * factor + jnp.sum(weights, axis=2)
    update = jnp.einsum(
        "hqk,khd->qhd", weights.astype(jnp.bfloat16), value_rows, preferred_element_type=jnp.float32
    )
    accum = accum * factor.T[:, :, None] + update
    return (new_max, totals, accum)


def merge_pair(earlier, later):
    return (earlier[0] + later[0], jnp.exp(later[0])[:, None] * earlier[1] + later[1])


def carry_in(log_total, flat_state):
    identity_pair = (jnp.zeros_like(log_total), jnp.zeros_like(flat_state))
    inner = carried_in((log_total, flat_state), "space", merge_pair, identity_pair)
    frame_whole = merge_pair(inner, (log_total, flat_state))
    last_index = lax.axis_size("space") - 1
    frame_sum = (
        from_root(for_sending(frame_whole[0]), "space", last_index),
        from_root(for_sending(frame_whole[1]), "space", last_index),
    )
    before = prefix(frame_sum, "tm", merge_pair, identity_pair)
    return merge_pair(before, inner)


def scan_terms(inner_rows, bc_rows, log_rates):
    b_proj = bc_rows[:, :STATE_DIM]
    c_proj = bc_rows[:, STATE_DIM:]
    length = inner_rows.shape[0]
    cumlog = jnp.cumsum(log_rates, axis=1)
    log_total = cumlog[:, -1]
    weights = (
        jnp.exp(log_total[:, None] - cumlog)[:, :, None] * b_proj.astype(jnp.float32)[None]
    ).astype(jnp.bfloat16)
    local_state = jnp.einsum(
        "hjn,jhp->hnp", weights, inner_rows, preferred_element_type=jnp.float32
    )
    pair_scores = jnp.dot(c_proj, b_proj.T, preferred_element_type=jnp.float32)
    lower_mask = (
        jnp.arange(length, dtype=jnp.int32)[:, None] >= jnp.arange(length, dtype=jnp.int32)[None, :]
    )
    log_gap = jnp.where(lower_mask[None], cumlog[:, :, None] - cumlog[:, None, :], FLOOR)
    mixer = (pair_scores[None] * jnp.exp(log_gap)).astype(jnp.bfloat16)
    inside = jnp.einsum("hij,jhp->ihp", mixer, inner_rows, preferred_element_type=jnp.float32)
    return (
        inside,
        cumlog,
        log_total,
        local_state.reshape(SCAN_HEADS, STATE_DIM * SCAN_DIM),
        c_proj,
    )


def scan_finish(inside, cumlog, c_proj, carried_flat):
    carried = carried_flat.reshape(SCAN_HEADS, STATE_DIM, SCAN_DIM)
    carried_out = jnp.einsum(
        "in,hnp->ihp", c_proj.astype(jnp.float32), carried, precision=lax.Precision.HIGHEST
    )
    return inside + jnp.exp(cumlog).T[:, :, None] * carried_out


def col_major(grid):
    return grid.transpose(1, 0, 2).reshape(grid.shape[0] * grid.shape[1], grid.shape[2])


def on_device(queries, keys, values, tile_mask, inner_x, bc_proj, log_decay, col_order, norm_gain):
    tokens = queries.shape[0]
    frame_idx = lax.axis_index("tm")
    frame_count = lax.axis_size("tm")
    reach = frame_count // 4
    score_scale = HEAD_DIM ** (-0.5)
    query_rows = queries.reshape(tokens, HEADS, HEAD_DIM)
    mask_row = lax.dynamic_index_in_dim(tile_mask, frame_idx, 0, keepdims=False)
    start_state = (
        jnp.full((HEADS, tokens), FLOOR, jnp.float32),
        jnp.zeros((HEADS, tokens), jnp.float32),
        jnp.zeros((tokens, HEADS, HEAD_DIM), jnp.float32),
    )

    def frame_allowed(other_frame):
        flag = lax.dynamic_index_in_dim(mask_row, other_frame % frame_count, 0, keepdims=False) > 0
        return jnp.broadcast_to(flag, (tokens,))

    kv_pair = jnp.stack([keys, values])
    far_pair = shifted(kv_pair, "tm", -reach)
    far_state = absorb(
        start_state,
        query_rows,
        far_pair[0],
        far_pair[1],
        frame_allowed(frame_idx + reach),
        score_scale,
    )

    def walk(distance, loop_state):
        pair_now, flash_now = loop_state
        pair_now = shifted(pair_now, "tm", 1)
        flash_now = absorb(
            flash_now,
            query_rows,
            pair_now[0],
            pair_now[1],
            frame_allowed(frame_idx + reach - distance + frame_count),
            score_scale,
        )
        return (pair_now, flash_now)

    _, flash_state = lax.fori_loop(1, 2 * reach + 1, walk, (far_pair, far_state))
    attention = (flash_state[2] / flash_state[1].T[:, :, None]).reshape(tokens, HEADS * HEAD_DIM)
    log_rates = log_decay.astype(jnp.float32)
    row_inside, row_cum, row_total, row_local, row_c = scan_terms(
        inner_x.reshape(tokens, SCAN_HEADS, SCAN_DIM), bc_proj, log_rates
    )
    grid_x = inner_x.reshape(ROWS_DEV, COLS, SCAN_HEADS * SCAN_DIM)[:, col_order]
    grid_bc = bc_proj.reshape(ROWS_DEV, COLS, 2 * STATE_DIM)[:, col_order]
    grid_log = log_decay.T.reshape(ROWS_DEV, COLS, SCAN_HEADS)[:, col_order]
    moved_x, moved_bc, moved_log = (
        lax.all_to_all(grid_x, "space", split_axis=1, concat_axis=0, tiled=True),
        lax.all_to_all(grid_bc, "space", split_axis=1, concat_axis=0, tiled=True),
        lax.all_to_all(grid_log, "space", split_axis=1, concat_axis=0, tiled=True),
    )
    height = moved_x.shape[0]
    col_part = moved_x.shape[1]
    col_inside, col_cum, col_total, col_local, col_c = scan_terms(
        col_major(moved_x).reshape(tokens, SCAN_HEADS, SCAN_DIM),
        col_major(moved_bc),
        col_major(moved_log).T.astype(jnp.float32),
    )
    both_total = jnp.concatenate([row_total, col_total], axis=0)
    both_local = jnp.concatenate([row_local, col_local], axis=0)
    prior = carry_in(both_total, both_local)[1]
    row_out = scan_finish(row_inside, row_cum, row_c, prior[:SCAN_HEADS])
    col_scan = scan_finish(col_inside, col_cum, col_c, prior[SCAN_HEADS:])
    back_rows = (
        col_scan.astype(jnp.bfloat16)
        .reshape(col_part, height, SCAN_HEADS * SCAN_DIM)
        .transpose(1, 0, 2)
    )
    returned = lax.all_to_all(back_rows, "space", split_axis=0, concat_axis=1, tiled=True)
    col_rows = jnp.zeros_like(returned).at[:, col_order].set(returned)
    col_rows = col_rows.reshape(tokens, SCAN_HEADS, SCAN_DIM).astype(jnp.float32)
    combined = row_out + col_rows
    meansq = jnp.mean(combined * combined, axis=2, keepdims=True)
    normed = combined * lax.rsqrt(meansq + EPS) * norm_gain.reshape(SCAN_HEADS, SCAN_DIM)
    return (attention + normed.reshape(tokens, SCAN_HEADS * SCAN_DIM)).astype(jnp.bfloat16)


def solution(mesh):
    return jax.shard_map(
        on_device,
        mesh=mesh,
        in_specs=(
            P(("tm", "space"), None),
            P(("tm", "space"), None),
            P(("tm", "space"), None),
            P(),
            P(("tm", "space"), None),
            P(("tm", "space"), None),
            P(None, ("tm", "space")),
            P(),
            P(),
        ),
        out_specs=P(("tm", "space"), None),
        check_vma=False,
    )
```

profile of v0, /device:TPU:8, one launch (start us, length us, event | category | flops | bytes accessed | tf_op | source)
XLA Modules:
  0.0 680.7 jit_solution(16776861308591096859)
XLA Ops:
  9.4 5.8 all-to-all-start
  15.3 1.2 copy.186
  16.5 1.3 copy.195
  17.8 1.6 gather_fusion.2
  21.1 5.7 all-to-all-start.1
  28.3 3.3 all-to-all-done.1
  31.6 4.8 all-to-all-start.2
  37.9 4.8 all-to-all-done.2
  45.8 15.5 %all-gather = bf16[8,1,48]{2,1,0:T(2,128)(2,1)S(1)} all-gather(bf16[1,1,48]{2,1,0:T(2,128)(2,1)S(1)} %maximum_bitcast_fusion), channel_id=1, replica_groups=mesh['tm'=32,'space'=8] {'space'}, dimensions={0}, use_global_device_ids=true | all-gather | bytes 864 | tf_op jit(solution)/shard_map/all_gather | solution.py:22
  62.0 57.7 %all-gather.5.cloned.1.call-done = bf16[8,48,4096]{2,1,0:T(8,128)(2,1)} async-done(((bf16[1,48,4096]{2,1,0:T(8,128)(2,1)}), bf16[8,48,4096]{2,1,0:T(8,128)(2,1)}) %all-gather.5.cloned.1.call-update) | async-done | bytes 3145744 | tf_op jit(solution)/shard_map/all_gather | solution.py:22
  119.8 2.5 while.46
  119.9 1.2 convert_add_fusion.3
  121.1 1.2 convert_add_fusion.3
  123.4 84.8 %all-reduce.2.cloned.1.call-done = bf16[1,48,4096]{2,1,0:T(8,128)(2,1)} async-done(((bf16[1,48,4096]{2,1,0:T(8,128)(2,1)}), bf16[1,48,4096]{2,1,0:T(8,128)(2,1)}) %all-reduce.2.cloned.1.call-update) | async-done | bytes 393232 | tf_op jit(solution)/shard_map/psum | solution.py:49
  208.8 7.9 %collective-permute-start.1 = (bf16[2,128,1536]{1,2,0:T(8,128)(2,1)S(1)}, bf16[2,128,1536]{1,2,0:T(8,128)(2,1)}, u32[]{:S(2)}, u32[]{:S(2)}) collective-permute-start(bf16[2,128,1536]{1,2,0:T(8,128)(2,1)S(1)} %pad_maximum_fusion), channel_id=1, source_target_pairs={{0,192},{8,200},{16,208},{24,216},{32,224},{40,232},{48,240},{56,2... | collective-permute-start | bytes 2359304 | tf_op jit(solution)/shard_map/ppermute | solution.py:76
  217.4 1.2 copy.176
  218.9 1.3 dynamic_slice.36
  220.8 1.3 dynamic-slice_bitcast_fusion
  222.3 1.7 convolution_bitcast_fusion.2
  224.8 30.3 %collective-permute-done.1 = bf16[2,128,1536]{1,2,0:T(8,128)(2,1)} collective-permute-done((bf16[2,128,1536]{1,2,0:T(8,128)(2,1)S(1)}, bf16[2,128,1536]{1,2,0:T(8,128)(2,1)}, u32[]{:S(2)}, u32[]{:S(2)}) %collective-permute-start.1) | collective-permute-done | bytes 786464 | tf_op jit(solution)/shard_map/ppermute | solution.py:76
  257.4 16.0 %psum.14 = bf16[1,48]{1,0:T(2,128)(2,1)S(1)} all-reduce(bf16[1,48]{1,0:T(2,128)(2,1)S(1)} %fusion.56), channel_id=1, replica_groups=mesh['tm'=32,'space'=8] {'space'}, use_global_device_ids=true, to_apply=%region_10.11 | all-reduce | flops 48 | bytes 192 | tf_op jit(solution)/shard_map/psum | solution.py:49
  273.4 40.7 %all-gather.1 = bf16[32,1,48]{2,1,0:T(2,128)(2,1)S(1)} all-gather(bf16[1,1,48]{2,1,0:T(2,128)(2,1)S(1)} %bitcast.201), channel_id=1, replica_groups=mesh['tm'=32,'space'=8] {'tm'}, dimensions={0}, use_global_device_ids=true | all-gather | bytes 3168 | tf_op jit(solution)/shard_map/all_gather | solution.py:55
  314.2 24.6 %all-gather.7.cloned.1.call-done = bf16[32,48,4096]{2,1,0:T(8,128)(2,1)} async-done(((bf16[1,48,4096]{2,1,0:T(8,128)(2,1)}), bf16[32,48,4096]{2,1,0:T(8,128)(2,1)}) %all-gather.7.cloned.1.call-update) | async-done | bytes 12582928 | tf_op jit(solution)/shard_map/all_gather | solution.py:55
  339.9 1.3 fusion.47
  341.3 1.5 fusion.17
  342.8 1.4 copy.203
  345.7 4.8 all-to-all-start.3
  350.5 313.6 %while.45 = (s32[]{:T(128)}, bf16[2,128,1536]{1,2,0:T(8,128)(2,1)}, f32[12,128]{1,0:T(8,128)S(1)}, f32[12,128]{1,0:T(8,128)S(1)}, f32[128,12,128]{2,0,1:T(8,128)...) while((s32[]{:T(128)}, bf16[2,128,1536]{1,2,0:T(8,128)(2,1)}, ...), condition=%wide.region_5.6_spmd, body=%wide.region_2.5_spmd.sunk | while | flops 102830608 | bytes 11501924 | solution.py:199
  352.7 47.2 %collective-permute-done = bf16[2,128,1536]{1,2,0:T(8,128)(2,1)S(1)} collective-permute-done((bf16[2,128,1536]{1,2,0:T(8,128)(2,1)}, bf16[2,128,1536]{1,2,0:T(8,128)(2,1)S(1)}, u32[]{:S(2)}, u32[]{:S(2)}) %collective-permute-start) | collective-permute-done | bytes 786464 | tf_op jit(solution)/shard_map/while/body/eval_jaxpr/ppermute | solution.py:76
  403.3 14.0 %collective-permute-done = bf16[2,128,1536]{1,2,0:T(8,128)(2,1)S(1)} collective-permute-done((bf16[2,128,1536]{1,2,0:T(8,128)(2,1)}, bf16[2,128,1536]{1,2,0:T(8,128)(2,1)S(1)}, u32[]{:S(2)}, u32[]{:S(2)}) %collective-permute-start) | collective-permute-done | bytes 786464 | tf_op jit(solution)/shard_map/while/body/eval_jaxpr/ppermute | solution.py:76
  420.8 14.0 %collective-permute-done = bf16[2,128,1536]{1,2,0:T(8,128)(2,1)S(1)} collective-permute-done((bf16[2,128,1536]{1,2,0:T(8,128)(2,1)}, bf16[2,128,1536]{1,2,0:T(8,128)(2,1)S(1)}, u32[]{:S(2)}, u32[]{:S(2)}) %collective-permute-start) | collective-permute-done | bytes 786464 | tf_op jit(solution)/shard_map/while/body/eval_jaxpr/ppermute | solution.py:76
  438.3 14.0 %collective-permute-done = bf16[2,128,1536]{1,2,0:T(8,128)(2,1)S(1)} collective-permute-done((bf16[2,128,1536]{1,2,0:T(8,128)(2,1)}, bf16[2,128,1536]{1,2,0:T(8,128)(2,1)S(1)}, u32[]{:S(2)}, u32[]{:S(2)}) %collective-permute-start) | collective-permute-done | bytes 786464 | tf_op jit(solution)/shard_map/while/body/eval_jaxpr/ppermute | solution.py:76
  455.8 14.0 %collective-permute-done = bf16[2,128,1536]{1,2,0:T(8,128)(2,1)S(1)} collective-permute-done((bf16[2,128,1536]{1,2,0:T(8,128)(2,1)}, bf16[2,128,1536]{1,2,0:T(8,128)(2,1)S(1)}, u32[]{:S(2)}, u32[]{:S(2)}) %collective-permute-start) | collective-permute-done | bytes 786464 | tf_op jit(solution)/shard_map/while/body/eval_jaxpr/ppermute | solution.py:76
  473.2 14.0 %collective-permute-done = bf16[2,128,1536]{1,2,0:T(8,128)(2,1)S(1)} collective-permute-done((bf16[2,128,1536]{1,2,0:T(8,128)(2,1)}, bf16[2,128,1536]{1,2,0:T(8,128)(2,1)S(1)}, u32[]{:S(2)}, u32[]{:S(2)}) %collective-permute-start) | collective-permute-done | bytes 786464 | tf_op jit(solution)/shard_map/while/body/eval_jaxpr/ppermute | solution.py:76
  490.7 14.0 %collective-permute-done = bf16[2,128,1536]{1,2,0:T(8,128)(2,1)S(1)} collective-permute-done((bf16[2,128,1536]{1,2,0:T(8,128)(2,1)}, bf16[2,128,1536]{1,2,0:T(8,128)(2,1)S(1)}, u32[]{:S(2)}, u32[]{:S(2)}) %collective-permute-start) | collective-permute-done | bytes 786464 | tf_op jit(solution)/shard_map/while/body/eval_jaxpr/ppermute | solution.py:76
  508.2 14.0 %collective-permute-done = bf16[2,128,1536]{1,2,0:T(8,128)(2,1)S(1)} collective-permute-done((bf16[2,128,1536]{1,2,0:T(8,128)(2,1)}, bf16[2,128,1536]{1,2,0:T(8,128)(2,1)S(1)}, u32[]{:S(2)}, u32[]{:S(2)}) %collective-permute-start) | collective-permute-done | bytes 786464 | tf_op jit(solution)/shard_map/while/body/eval_jaxpr/ppermute | solution.py:76
  525.6 14.0 %collective-permute-done = bf16[2,128,1536]{1,2,0:T(8,128)(2,1)S(1)} collective-permute-done((bf16[2,128,1536]{1,2,0:T(8,128)(2,1)}, bf16[2,128,1536]{1,2,0:T(8,128)(2,1)S(1)}, u32[]{:S(2)}, u32[]{:S(2)}) %collective-permute-start) | collective-permute-done | bytes 786464 | tf_op jit(solution)/shard_map/while/body/eval_jaxpr/ppermute | solution.py:76
  543.1 14.0 %collective-permute-done = bf16[2,128,1536]{1,2,0:T(8,128)(2,1)S(1)} collective-permute-done((bf16[2,128,1536]{1,2,0:T(8,128)(2,1)}, bf16[2,128,1536]{1,2,0:T(8,128)(2,1)S(1)}, u32[]{:S(2)}, u32[]{:S(2)}) %collective-permute-start) | collective-permute-done | bytes 786464 | tf_op jit(solution)/shard_map/while/body/eval_jaxpr/ppermute | solution.py:76
  560.6 14.0 %collective-permute-done = bf16[2,128,1536]{1,2,0:T(8,128)(2,1)S(1)} collective-permute-done((bf16[2,128,1536]{1,2,0:T(8,128)(2,1)}, bf16[2,128,1536]{1,2,0:T(8,128)(2,1)S(1)}, u32[]{:S(2)}, u32[]{:S(2)}) %collective-permute-start) | collective-permute-done | bytes 786464 | tf_op jit(solution)/shard_map/while/body/eval_jaxpr/ppermute | solution.py:76
  578.0 14.0 %collective-permute-done = bf16[2,128,1536]{1,2,0:T(8,128)(2,1)S(1)} collective-permute-done((bf16[2,128,1536]{1,2,0:T(8,128)(2,1)}, bf16[2,128,1536]{1,2,0:T(8,128)(2,1)S(1)}, u32[]{:S(2)}, u32[]{:S(2)}) %collective-permute-start) | collective-permute-done | bytes 786464 | tf_op jit(solution)/shard_map/while/body/eval_jaxpr/ppermute | solution.py:76
  595.5 14.0 %collective-permute-done = bf16[2,128,1536]{1,2,0:T(8,128)(2,1)S(1)} collective-permute-done((bf16[2,128,1536]{1,2,0:T(8,128)(2,1)}, bf16[2,128,1536]{1,2,0:T(8,128)(2,1)S(1)}, u32[]{:S(2)}, u32[]{:S(2)}) %collective-permute-start) | collective-permute-done | bytes 786464 | tf_op jit(solution)/shard_map/while/body/eval_jaxpr/ppermute | solution.py:76
  613.0 14.0 %collective-permute-done = bf16[2,128,1536]{1,2,0:T(8,128)(2,1)S(1)} collective-permute-done((bf16[2,128,1536]{1,2,0:T(8,128)(2,1)}, bf16[2,128,1536]{1,2,0:T(8,128)(2,1)S(1)}, u32[]{:S(2)}, u32[]{:S(2)}) %collective-permute-start) | collective-permute-done | bytes 786464 | tf_op jit(solution)/shard_map/while/body/eval_jaxpr/ppermute | solution.py:76
  630.5 14.0 %collective-permute-done = bf16[2,128,1536]{1,2,0:T(8,128)(2,1)S(1)} collective-permute-done((bf16[2,128,1536]{1,2,0:T(8,128)(2,1)}, bf16[2,128,1536]{1,2,0:T(8,128)(2,1)S(1)}, u32[]{:S(2)}, u32[]{:S(2)}) %collective-permute-start) | collective-permute-done | bytes 786464 | tf_op jit(solution)/shard_map/while/body/eval_jaxpr/ppermute | solution.py:76
  647.9 14.0 %collective-permute-done = bf16[2,128,1536]{1,2,0:T(8,128)(2,1)S(1)} collective-permute-done((bf16[2,128,1536]{1,2,0:T(8,128)(2,1)}, bf16[2,128,1536]{1,2,0:T(8,128)(2,1)S(1)}, u32[]{:S(2)}, u32[]{:S(2)}) %collective-permute-start) | collective-permute-done | bytes 786464 | tf_op jit(solution)/shard_map/while/body/eval_jaxpr/ppermute | solution.py:76
  665.1 1.5 scatter_fusion
  667.6 1.5 reshape.244
  669.2 1.4 copy.207
  670.6 2.2 multiply_reduce_fusion
  (285 shorter events, 69.2 us)
Async XLA Ops:
  6.5 12.9 %copy-start.10 = (bf16[24,128]{1,0:T(8,128)(2,1)S(1)}, bf16[24,128]{1,0:T(8,128)(2,1)}, u32[]{:S(2)}) copy-start(bf16[24,128]{1,0:T(8,128)(2,1)} %param.21) | copy-start | bytes 18436
  6.5 13.2 %copy-start = (bf16[128,128]{1,0:T(8,128)(2,1)S(1)}, bf16[128,128]{1,0:T(8,128)(2,1)}, u32[]{:S(2)}) copy-start(bf16[128,128]{1,0:T(8,128)(2,1)} %param.20) | copy-start | bytes 98308
  7.2 12.5 %copy-start.15 = (s32[32]{0:T(128)}, s32[32]{0:T(128)S(1)}, u32[]{:S(2)}) copy-start(s32[32]{0:T(128)S(1)} %compare_select_fusion) | copy-start | bytes 388
  9.4 11.6 %all-to-all-start = ((bf16[8,2,192]{2,1,0:T(2,128)(2,1)}), bf16[8,2,192]{2,1,0:T(2,128)(2,1)S(1)}, u32[]{:S(2)}, u32[]{:S(2)}) async-start(bf16[8,2,192]{2,1,0:T(2,128)(2,1)} %reshape.295), calls=%async_computation | async-start | bytes 16384 | tf_op jit(solution)/shard_map/all_to_all | solution.py:211
  21.1 10.5 %all-to-all-start.1 = ((bf16[4,32,128]{2,0,1:T(4,128)(2,1)}), bf16[4,32,128]{2,0,1:T(4,128)(2,1)S(1)}, u32[]{:S(2)}, u32[]{:S(2)}) async-start(bf16[4,32,128]{2,0,1:T(4,128)(2,1)} %bitcast.35), calls=%async_computation.1 | async-start | bytes 65536 | tf_op jit(solution)/shard_map/all_to_all | solution.py:210
  27.5 18.1 %copy-start.5 = (f32[24,128]{1,0:T(8,128)}, f32[24,128]{1,0:T(8,128)S(1)}, u32[]{:S(2)}) copy-start(f32[24,128]{1,0:T(8,128)S(1)} %reduce_window_sum.18) | copy-start | bytes 36868
  31.6 11.1 %all-to-all-start.2 = ((bf16[4,32,1536]{2,0,1:T(4,128)(2,1)}), bf16[4,32,1536]{2,0,1:T(4,128)(2,1)S(1)}, u32[]{:S(2)}, u32[]{:S(2)}) async-start(bf16[4,32,1536]{2,0,1:T(4,128)(2,1)} %bitcast.42), calls=%async_computation.2 | async-start | bytes 786432 | tf_op jit(solution)/shard_map/all_to_all | solution.py:209
  36.4 83.4 %all-gather.5.cloned.1.call-start = ((), (), s32[]{:S(2)}) async-start(), calls=%async_computation.4 | async-start | bytes 3538944 | tf_op jit(solution)/shard_map/all_gather | solution.py:22
  37.7 186.3 %copy-start.2 = (bf16[4,8,4,128]{3,0,1,2:T(4,128)(2,1)}, bf16[4,8,4,128]{3,0,1,2:T(4,128)(2,1)S(1)}, u32[]{:S(2)}) copy-start(bf16[4,8,4,128]{3,0,1,2:T(4,128)(2,1)S(1)} %copy.193) | copy-start | bytes 98308
  45.3 162.9 %all-reduce.2.cloned.1.call-start = ((), (), s32[]{:S(2)}) async-start(), calls=%async_computation.5 | async-start | bytes 786432 | tf_op jit(solution)/shard_map/psum | solution.py:49
  122.4 85.9 %copy-start.3 = (bf16[128,1536]{1,0:T(8,128)(2,1)S(1)}, bf16[128,1536]{1,0:T(8,128)(2,1)}, u32[]{:S(2)}) copy-start(bf16[128,1536]{1,0:T(8,128)(2,1)} %param.17) | copy-start | bytes 1179652
  123.3 85.2 %copy-start.4 = (bf16[128,1536]{1,0:T(8,128)(2,1)S(1)}, bf16[128,1536]{1,0:T(8,128)(2,1)}, u32[]{:S(2)}) copy-start(bf16[128,1536]{1,0:T(8,128)(2,1)} %param.16) | copy-start | bytes 1179652
  123.3 215.5 %all-gather.7.cloned.1.call-start = ((), (), s32[]{:S(2)}) async-start(), calls=%async_computation.6 | async-start | bytes 12976128 | tf_op jit(solution)/shard_map/all_gather | solution.py:55
  208.2 8.5 %copy-start.14 = (f32[1536]{0:T(1024)S(1)}, f32[1536]{0:T(1024)}, u32[]{:S(2)}) copy-start(f32[1536]{0:T(1024)} %param.23) | copy-start | bytes 18436
  208.8 46.3 %collective-permute-start.1 = (bf16[2,128,1536]{1,2,0:T(8,128)(2,1)S(1)}, bf16[2,128,1536]{1,2,0:T(8,128)(2,1)}, u32[]{:S(2)}, u32[]{:S(2)}) collective-permute-start(bf16[2,128,1536]{1,2,0:T(8,128)(2,1)S(1)} %pad_maximum_fusion), channel_id=1, source_target_pairs={{0,192},{8,200},{16,208},{24,216},{32,224},{40,232},{48,240},{56,2... | collective-permute-start | bytes 2359304 | tf_op jit(solution)/shard_map/ppermute | solution.py:76
  220.8 35.4 %copy-start.11 = (pred[128,128]{1,0:T(8,128)(4,1)}, pred[128,128]{1,0:T(8,128)(4,1)S(1)}, u32[]{:S(2)}) copy-start(pred[128,128]{1,0:T(8,128)(4,1)S(1)} %iota_compare_fusion) | copy-start | bytes 49156
  339.9 1.4 copy-start.6
  339.9 1.4 copy-start.7
  339.9 1.4 copy-start.12
  339.9 1.4 copy-start.13
  344.2 6.3 copy-start.17
  345.7 319.1 %all-to-all-start.3 = ((bf16[32,4,1536]{2,1,0:T(4,128)(2,1)}), bf16[32,4,1536]{2,1,0:T(4,128)(2,1)S(1)}, u32[]{:S(2)}, u32[]{:S(2)}) async-start(bf16[32,4,1536]{2,1,0:T(4,128)(2,1)} %copy.204), calls=%async_computation.3 | async-start | bytes 786432 | tf_op jit(solution)/shard_map/all_to_all | solution.py:230
  350.5 49.3 %collective-permute-start = (bf16[2,128,1536]{1,2,0:T(8,128)(2,1)}, bf16[2,128,1536]{1,2,0:T(8,128)(2,1)S(1)}, u32[]{:S(2)}, u32[]{:S(2)}) collective-permute-start(bf16[2,128,1536]{1,2,0:T(8,128)(2,1)} %get-tuple-element.604), channel_id=1, source_target_pairs={{0,8},{8,16},{16,24},{24,32},{32,40},{40,48},{48,56},{56,64},{64,7... | collective-permute-start | bytes 2359304 | tf_op jit(solution)/shard_map/while/body/eval_jaxpr/ppermute | solution.py:76
  402.1 15.2 %collective-permute-start = (bf16[2,128,1536]{1,2,0:T(8,128)(2,1)}, bf16[2,128,1536]{1,2,0:T(8,128)(2,1)S(1)}, u32[]{:S(2)}, u32[]{:S(2)}) collective-permute-start(bf16[2,128,1536]{1,2,0:T(8,128)(2,1)} %get-tuple-element.604), channel_id=1, source_target_pairs={{0,8},{8,16},{16,24},{24,32},{32,40},{40,48},{48,56},{56,64},{64,7... | collective-permute-start | bytes 2359304 | tf_op jit(solution)/shard_map/while/body/eval_jaxpr/ppermute | solution.py:76
  419.5 15.2 %collective-permute-start = (bf16[2,128,1536]{1,2,0:T(8,128)(2,1)}, bf16[2,128,1536]{1,2,0:T(8,128)(2,1)S(1)}, u32[]{:S(2)}, u32[]{:S(2)}) collective-permute-start(bf16[2,128,1536]{1,2,0:T(8,128)(2,1)} %get-tuple-element.604), channel_id=1, source_target_pairs={{0,8},{8,16},{16,24},{24,32},{32,40},{40,48},{48,56},{56,64},{64,7... | collective-permute-start | bytes 2359304 | tf_op jit(solution)/shard_map/while/body/eval_jaxpr/ppermute | solution.py:76
  437.0 15.2 %collective-permute-start = (bf16[2,128,1536]{1,2,0:T(8,128)(2,1)}, bf16[2,128,1536]{1,2,0:T(8,128)(2,1)S(1)}, u32[]{:S(2)}, u32[]{:S(2)}) collective-permute-start(bf16[2,128,1536]{1,2,0:T(8,128)(2,1)} %get-tuple-element.604), channel_id=1, source_target_pairs={{0,8},{8,16},{16,24},{24,32},{32,40},{40,48},{48,56},{56,64},{64,7... | collective-permute-start | bytes 2359304 | tf_op jit(solution)/shard_map/while/body/eval_jaxpr/ppermute | solution.py:76
  454.5 15.2 %collective-permute-start = (bf16[2,128,1536]{1,2,0:T(8,128)(2,1)}, bf16[2,128,1536]{1,2,0:T(8,128)(2,1)S(1)}, u32[]{:S(2)}, u32[]{:S(2)}) collective-permute-start(bf16[2,128,1536]{1,2,0:T(8,128)(2,1)} %get-tuple-element.604), channel_id=1, source_target_pairs={{0,8},{8,16},{16,24},{24,32},{32,40},{40,48},{48,56},{56,64},{64,7... | collective-permute-start | bytes 2359304 | tf_op jit(solution)/shard_map/while/body/eval_jaxpr/ppermute | solution.py:76
  471.9 15.2 %collective-permute-start = (bf16[2,128,1536]{1,2,0:T(8,128)(2,1)}, bf16[2,128,1536]{1,2,0:T(8,128)(2,1)S(1)}, u32[]{:S(2)}, u32[]{:S(2)}) collective-permute-start(bf16[2,128,1536]{1,2,0:T(8,128)(2,1)} %get-tuple-element.604), channel_id=1, source_target_pairs={{0,8},{8,16},{16,24},{24,32},{32,40},{40,48},{48,56},{56,64},{64,7... | collective-permute-start | bytes 2359304 | tf_op jit(solution)/shard_map/while/body/eval_jaxpr/ppermute | solution.py:76
  489.4 15.2 %collective-permute-start = (bf16[2,128,1536]{1,2,0:T(8,128)(2,1)}, bf16[2,128,1536]{1,2,0:T(8,128)(2,1)S(1)}, u32[]{:S(2)}, u32[]{:S(2)}) collective-permute-start(bf16[2,128,1536]{1,2,0:T(8,128)(2,1)} %get-tuple-element.604), channel_id=1, source_target_pairs={{0,8},{8,16},{16,24},{24,32},{32,40},{40,48},{48,56},{56,64},{64,7... | collective-permute-start | bytes 2359304 | tf_op jit(solution)/shard_map/while/body/eval_jaxpr/ppermute | solution.py:76
  506.9 15.2 %collective-permute-start = (bf16[2,128,1536]{1,2,0:T(8,128)(2,1)}, bf16[2,128,1536]{1,2,0:T(8,128)(2,1)S(1)}, u32[]{:S(2)}, u32[]{:S(2)}) collective-permute-start(bf16[2,128,1536]{1,2,0:T(8,128)(2,1)} %get-tuple-element.604), channel_id=1, source_target_pairs={{0,8},{8,16},{16,24},{24,32},{32,40},{40,48},{48,56},{56,64},{64,7... | collective-permute-start | bytes 2359304 | tf_op jit(solution)/shard_map/while/body/eval_jaxpr/ppermute | solution.py:76
  524.3 15.2 %collective-permute-start = (bf16[2,128,1536]{1,2,0:T(8,128)(2,1)}, bf16[2,128,1536]{1,2,0:T(8,128)(2,1)S(1)}, u32[]{:S(2)}, u32[]{:S(2)}) collective-permute-start(bf16[2,128,1536]{1,2,0:T(8,128)(2,1)} %get-tuple-element.604), channel_id=1, source_target_pairs={{0,8},{8,16},{16,24},{24,32},{32,40},{40,48},{48,56},{56,64},{64,7... | collective-permute-start | bytes 2359304 | tf_op jit(solution)/shard_map/while/body/eval_jaxpr/ppermute | solution.py:76
  541.8 15.2 %collective-permute-start = (bf16[2,128,1536]{1,2,0:T(8,128)(2,1)}, bf16[2,128,1536]{1,2,0:T(8,128)(2,1)S(1)}, u32[]{:S(2)}, u32[]{:S(2)}) collective-permute-start(bf16[2,128,1536]{1,2,0:T(8,128)(2,1)} %get-tuple-element.604), channel_id=1, source_target_pairs={{0,8},{8,16},{16,24},{24,32},{32,40},{40,48},{48,56},{56,64},{64,7... | collective-permute-start | bytes 2359304 | tf_op jit(solution)/shard_map/while/body/eval_jaxpr/ppermute | solution.py:76
  559.3 15.2 %collective-permute-start = (bf16[2,128,1536]{1,2,0:T(8,128)(2,1)}, bf16[2,128,1536]{1,2,0:T(8,128)(2,1)S(1)}, u32[]{:S(2)}, u32[]{:S(2)}) collective-permute-start(bf16[2,128,1536]{1,2,0:T(8,128)(2,1)} %get-tuple-element.604), channel_id=1, source_target_pairs={{0,8},{8,16},{16,24},{24,32},{32,40},{40,48},{48,56},{56,64},{64,7... | collective-permute-start | bytes 2359304 | tf_op jit(solution)/shard_map/while/body/eval_jaxpr/ppermute | solution.py:76
  576.8 15.2 %collective-permute-start = (bf16[2,128,1536]{1,2,0:T(8,128)(2,1)}, bf16[2,128,1536]{1,2,0:T(8,128)(2,1)S(1)}, u32[]{:S(2)}, u32[]{:S(2)}) collective-permute-start(bf16[2,128,1536]{1,2,0:T(8,128)(2,1)} %get-tuple-element.604), channel_id=1, source_target_pairs={{0,8},{8,16},{16,24},{24,32},{32,40},{40,48},{48,56},{56,64},{64,7... | collective-permute-start | bytes 2359304 | tf_op jit(solution)/shard_map/while/body/eval_jaxpr/ppermute | solution.py:76
  594.2 15.2 %collective-permute-start = (bf16[2,128,1536]{1,2,0:T(8,128)(2,1)}, bf16[2,128,1536]{1,2,0:T(8,128)(2,1)S(1)}, u32[]{:S(2)}, u32[]{:S(2)}) collective-permute-start(bf16[2,128,1536]{1,2,0:T(8,128)(2,1)} %get-tuple-element.604), channel_id=1, source_target_pairs={{0,8},{8,16},{16,24},{24,32},{32,40},{40,48},{48,56},{56,64},{64,7... | collective-permute-start | bytes 2359304 | tf_op jit(solution)/shard_map/while/body/eval_jaxpr/ppermute | solution.py:76
  611.7 15.2 %collective-permute-start = (bf16[2,128,1536]{1,2,0:T(8,128)(2,1)}, bf16[2,128,1536]{1,2,0:T(8,128)(2,1)S(1)}, u32[]{:S(2)}, u32[]{:S(2)}) collective-permute-start(bf16[2,128,1536]{1,2,0:T(8,128)(2,1)} %get-tuple-element.604), channel_id=1, source_target_pairs={{0,8},{8,16},{16,24},{24,32},{32,40},{40,48},{48,56},{56,64},{64,7... | collective-permute-start | bytes 2359304 | tf_op jit(solution)/shard_map/while/body/eval_jaxpr/ppermute | solution.py:76
  629.2 15.2 %collective-permute-start = (bf16[2,128,1536]{1,2,0:T(8,128)(2,1)}, bf16[2,128,1536]{1,2,0:T(8,128)(2,1)S(1)}, u32[]{:S(2)}, u32[]{:S(2)}) collective-permute-start(bf16[2,128,1536]{1,2,0:T(8,128)(2,1)} %get-tuple-element.604), channel_id=1, source_target_pairs={{0,8},{8,16},{16,24},{24,32},{32,40},{40,48},{48,56},{56,64},{64,7... | collective-permute-start | bytes 2359304 | tf_op jit(solution)/shard_map/while/body/eval_jaxpr/ppermute | solution.py:76
  646.6 15.2 %collective-permute-start = (bf16[2,128,1536]{1,2,0:T(8,128)(2,1)}, bf16[2,128,1536]{1,2,0:T(8,128)(2,1)S(1)}, u32[]{:S(2)}, u32[]{:S(2)}) collective-permute-start(bf16[2,128,1536]{1,2,0:T(8,128)(2,1)} %get-tuple-element.604), channel_id=1, source_target_pairs={{0,8},{8,16},{16,24},{24,32},{32,40},{40,48},{48,56},{56,64},{64,7... | collective-permute-start | bytes 2359304 | tf_op jit(solution)/shard_map/while/body/eval_jaxpr/ppermute | solution.py:76
  664.4 0.7 copy-start.16
  669.2 1.4 copy-start.1
  669.2 1.4 copy-start.9
  670.6 2.2 copy-start.8
Sparse Core Ops, SparseCore 0:
  45.5 74.2 all-gather.4
  123.4 84.7 all-reduce.1
  211.4 127.4 all-gather.6
where the time goes:
time: 683 us; the launch traced here: 681 us
  waiting for transfers between devices  462 us (68%)
  blocking collectives  72.3 us (11%)
  local copies, waits for them, and re-layouts  53.2 us (8%)
  starting transfers between devices  30.1 us (4%)
  matrix products  26.2 us (4%)
  between operations  14.3 us (2%)
  other arithmetic  11.5 us (2%)
  loops' own time  11.1 us (2%)
    ppermute x17, waiting for transfers between devices, shifted(): lax.ppermute(array, axis, [(i, (i + by) % devices) for i in range(devices)])  287 us
    psum x1, waiting for transfers between devices, from_root(): return lax.psum(jnp.where(mine, array, jnp.zeros_like(array)), axis)  84.8 us
    all_gather x1, waiting for transfers between devices, carried_in(): lax.all_gather(a.astype(kind), axis)  57.7 us
    all_gather x1, blocking collectives, prefix(): lax.all_gather(a.astype(kind), axis)  40.7 us
    all_gather x1, waiting for transfers between devices, prefix(): lax.all_gather(a.astype(kind), axis)  24.6 us
    psum x1, blocking collectives, from_root(): return lax.psum(jnp.where(mine, array, jnp.zeros_like(array)), axis)  16 us
    all_gather x1, blocking collectives, carried_in(): lax.all_gather(a.astype(kind), axis)  15.5 us
    while x32, local copies, waits for them, and re-layouts  14.4 us
  transfers between devices with their start and end apart: 24, of which 22 were waited for; matrix products, arithmetic and copies ran while one was open for 10% of the time, Pallas kernels for 0%

commit v1 on v0

v1 whole, which is shorter than its diff:
```python
import functools
import math

import jax
import jax.numpy as jnp
from jax import lax
from jax.experimental import pallas as pl
from jax.experimental.pallas import tpu as pltpu
from jax.sharding import PartitionSpec as P

HEADS = 12
HEAD_DIM = 128
SCAN_HEADS = 24
SCAN_DIM = 64
STATE_DIM = 64
COLS = 32
TOKENS = 128
N_TM = 32
N_SPACE = 8
GROUP = HEADS // 4 * HEAD_DIM
WIN = 256
ROWS = STATE_DIM + 8

EPS = 1e-05
FLOOR = -1e30
LOG2_SCALE = HEAD_DIM ** (-0.5) * math.log2(math.e)
BF16 = jnp.bfloat16
F32 = jnp.float32

VMEM = pl.BlockSpec(memory_space=pltpu.VMEM)
SMEM = pl.BlockSpec(memory_space=pltpu.SMEM)


def call(body, out_shape, n_smem, n_vmem, scratch=(), flops=0, moved=0, aliases=None):
    return pl.pallas_call(
        body,
        out_shape=out_shape,
        in_specs=[SMEM] * n_smem + [VMEM] * n_vmem,
        out_specs=jax.tree.map(lambda _: VMEM, out_shape),
        scratch_shapes=list(scratch),
        input_output_aliases=aliases or {},
        compiler_params=pltpu.CompilerParams(vmem_limit_bytes=24 * 2**20),
        cost_estimate=pl.CostEstimate(flops=flops, bytes_accessed=moved, transcendentals=0),
    )


def dot(a, b, contract=(1, 0)):
    return lax.dot_general(
        a, b, (((contract[0],), (contract[1],)), ((), ())), preferred_element_type=F32
    )


def iota(shape, axis):
    return lax.broadcasted_iota(jnp.int32, shape, axis)


def head_groups(ids, q_ref, k_ref, v_ref, *outs):
    group = ids[0]
    for i, out in enumerate(outs):
        cols = pl.ds(pl.multiple_of((group ^ i) * GROUP, 128), GROUP)
        out[0] = q_ref[:, cols]
        out[1] = k_ref[:, cols]
        out[2] = v_ref[:, cols]


def absorb(ids, mask_ref, q_ref, kv_ref, m_ref, l_ref, acc_ref, source, delta, query, first):
    group, place = ids[0], ids[1]
    half, core = group // 2, group % 2
    there = place + delta
    wrapped = jnp.where((there < 0) | (there > 7), 1, 0)
    there = there & 7
    u = source ^ wrapped if query is None else query
    if first:
        u = query
    lanes = iota((1, 2 * TOKENS), 1)

    def bias(j):
        frame_k = 16 * (half ^ source) + 2 * there + (core ^ j)

        def one(a):
            frame_q = 16 * (half ^ u) + 2 * place + (core ^ a)
            return jnp.where(mask_ref[frame_q, frame_k] > 0, 0.0, FLOOR).astype(F32)

        return jnp.where(lanes < TOKENS, one(0), one(1))

    bias0, bias1 = bias(0), bias(1)
    for h in range(GROUP // HEAD_DIM):
        cols = slice(h * HEAD_DIM, (h + 1) * HEAD_DIM)
        q = q_ref[u, :, :, cols].reshape(2 * TOKENS, HEAD_DIM)
        k = kv_ref[:, 0, :, cols].reshape(2 * TOKENS, HEAD_DIM)
        v = kv_ref[:, 1, :, cols].reshape(2 * TOKENS, HEAD_DIM)
        scores = dot(k, q, (1, 1))
        s0, s1 = scores[:TOKENS], scores[TOKENS:]
        top = jnp.maximum(
            jnp.max(s0, axis=0, keepdims=True) * LOG2_SCALE + bias0,
            jnp.max(s1, axis=0, keepdims=True) * LOG2_SCALE + bias1,
        )
        if not first:
            old = m_ref[u, h : h + 1, :]
            top = jnp.maximum(top, old)
        p0 = jnp.exp2(s0 * LOG2_SCALE + (bias0 - top))
        p1 = jnp.exp2(s1 * LOG2_SCALE + (bias1 - top))
        total = jnp.sum(p0 + p1, axis=0, keepdims=True)
        probs = jnp.concatenate([p0.astype(BF16), p1.astype(BF16)], axis=0)
        update = dot(v, probs, (0, 0))
        if first:
            l_ref[u, h : h + 1, :] = total
            acc_ref[u, h] = update
        else:
            factor = jnp.exp2(old - top)
            l_ref[u, h : h + 1, :] = l_ref[u, h : h + 1, :] * factor + total
            acc_ref[u, h] = acc_ref[u, h] * factor + update
        m_ref[u, h : h + 1, :] = top


STATE = (
    jax.ShapeDtypeStruct((2, 8, 2 * TOKENS), F32),
    jax.ShapeDtypeStruct((2, 8, 2 * TOKENS), F32),
    jax.ShapeDtypeStruct((2, HEADS // 4, HEAD_DIM, 2 * TOKENS), F32),
)
ITEM_FLOPS = 4 * 256 * 256 * 128 * 3


def attend_own(ids, mask_ref, q_ref, a_ref, b_ref, m_ref, l_ref, acc_ref):
    m_ref[...] = jnp.zeros_like(m_ref)
    l_ref[...] = jnp.zeros_like(l_ref)
    absorb(ids, mask_ref, q_ref, a_ref, m_ref, l_ref, acc_ref, 0, 0, 0, True)
    absorb(ids, mask_ref, q_ref, b_ref, m_ref, l_ref, acc_ref, 1, 0, 1, True)


def attend_pair(items, ids, mask_ref, q_ref, c0, c1, m_in, l_in, acc_in, m_ref, l_ref, acc_ref):
    m_ref[...] = m_in[...]
    l_ref[...] = l_in[...]
    acc_ref[...] = acc_in[...]
    for kv_ref, (source, delta, query) in zip((c0, c1), items):
        absorb(ids, mask_ref, q_ref, kv_ref, m_ref, l_ref, acc_ref, source, delta, query, False)


def attend_last(ids, mask_ref, q_ref, c0, c1, m_in, l_in, acc_in, *rest):
    outs, (m_ref, l_ref, acc_ref) = rest[:4], rest[4:]
    m_ref[...] = m_in[...]
    l_ref[...] = l_in[...]
    acc_ref[...] = acc_in[...]
    for u in range(2):
        for source, kv_ref in ((0, c0), (1, c1)):
            absorb(ids, mask_ref, q_ref, kv_ref, m_ref, l_ref, acc_ref, source, 4, u, False)
    for u in range(2):
        for h in range(GROUP // HEAD_DIM):
            out = acc_ref[u, h] / l_ref[u, h : h + 1, :]
            out = out.T.astype(BF16)
            cols = slice(h * HEAD_DIM, (h + 1) * HEAD_DIM)
            outs[2 * u][:, cols] = out[:TOKENS]
            outs[2 * u + 1][:, cols] = out[TOKENS:]


def scan_pack(x_ref, bc_ref, log_ref, out_ref):
    lanes = iota((TOKENS, WIN), 1)
    logs = log_ref[...]
    bc = bc_ref[...]
    head = iota((SCAN_HEADS, WIN), 0)
    lane = iota((SCAN_HEADS, WIN), 1)
    for s in range(N_SPACE):
        base = 384 * (s // 2) + 128 * (s % 2)
        free = 0 if s % 2 else 192
        pick = ((lane - free) == (head - 3 * s)) & (head >= 3 * s) & (head < 3 * s + 3)
        moved = dot(logs, jnp.where(pick, 1.0, 0.0).astype(BF16), (0, 0)).astype(BF16)
        window = x_ref[:, base : base + WIN]
        own = lanes >= 64 if s % 2 else lanes < 192
        out_ref[s, :, :WIN] = jnp.where(own, window, moved)
        out_ref[s, :, WIN:] = bc


def split_high(a):
    high = a.astype(BF16)
    return high, (a - high.astype(F32)).astype(BF16)


def scan_frame(ids, order_ref, in_ref, y_ref, row_ref, col_ref, state_ref, rows, cols):
    odd = ids[2] % 2
    free = jnp.where(odd == 1, 0, 192)
    for s in range(N_SPACE):
        for t in range(3):
            part = in_ref[s, :, t * 128 : (t + 1) * 128]
            rows[t, s * TOKENS : (s + 1) * TOKENS, :] = part.astype(F32)
    for k in range(COLS):
        for t in range(3):
            cols[t, k * 32 : (k + 1) * 32, :] = rows[t, pl.ds(order_ref[k], 32, stride=COLS), :]

    lane = iota((WIN, WIN), 1)
    spread = (iota((WIN, WIN), 0) == free + lane // 64 - odd) & (lane // 64 != free // 64)
    spread = jnp.where(spread, 1.0, 0.0).astype(BF16)
    wide = iota((WIN, 3 * TOKENS), 0) == free + iota((WIN, 3 * TOKENS), 1) // TOKENS
    wide = jnp.where(wide, 1.0, 0.0).astype(BF16)
    i, j = iota((TOKENS, TOKENS), 0), iota((TOKENS, TOKENS), 1)
    lower_mask = i >= j
    lower = jnp.where(lower_mask, 1.0, 0.0).astype(BF16)
    upper = jnp.where(i <= j, 1.0, 0.0).astype(BF16)
    group = iota((TOKENS, WIN), 1) // 64
    real = group != free // 64

    def block(buf, b, carry, before):
        start = pl.multiple_of(b * TOKENS, TOKENS)
        here = pl.ds(start, TOKENS)
        window = jnp.concatenate([buf[0, here, :], buf[1, here, :]], axis=1)
        bc = buf[2, here, :].astype(BF16)
        b_proj, c_proj = bc[:, :STATE_DIM], bc[:, STATE_DIM:]
        packed = window.astype(BF16)
        x = jnp.where(real, window, 0.0)
        log_lane = dot(packed, spread).astype(BF16)
        log_wide = dot(packed, wide).astype(BF16)
        cum = dot(lower, log_lane)
        cum_i = dot(lower, log_wide)
        scores = dot(c_proj, b_proj, (1, 1))
        mixers, parts = [], []
        for h in range(3):
            span = slice(h * TOKENS, (h + 1) * TOKENS)
            cum_j = dot(log_wide[:, span], upper, (0, 0))
            gap = jnp.where(lower_mask, cum_i[:, span] - cum_j, FLOOR)
            mixers.append((scores * jnp.exp(gap)).astype(BF16))
            parts.append(jnp.where(group == h + odd, x, 0.0).astype(BF16))
        inside = dot(jnp.concatenate(mixers, axis=1), jnp.concatenate(parts, axis=0))
        total = cum[TOKENS - 1 : TOKENS, :]
        local = dot(b_proj, (x * jnp.exp(total - cum)).astype(BF16), (0, 0))
        high, low = split_high(carry)
        carried = dot(c_proj, high) + dot(c_proj, low)
        out = inside + jnp.exp(cum) * carried
        return out, jnp.exp(cum + before), jnp.exp(total) * carry + local, before + total

    carry = jnp.zeros((STATE_DIM, WIN), F32)
    before = jnp.zeros((1, WIN), F32)

    def row_block(b, state):
        out, decay, carry, before = block(rows, b, *state)
        here = pl.ds(pl.multiple_of(b * TOKENS, TOKENS), TOKENS)
        for t in range(2):
            y_ref[t, here, :] = out[:, t * 128 : (t + 1) * 128]
            row_ref[t, here, :] = decay[:, t * 128 : (t + 1) * 128]
        return carry, before

    def col_block(b, state):
        out, decay, carry, before = block(cols, b, *state)
        for k in range(TOKENS // 32):
            here = pl.ds(order_ref[b * 4 + k], 32, stride=COLS)
            span = slice(k * 32, (k + 1) * 32)
            for t in range(2):
                lanes = slice(t * 128, (t + 1) * 128)
                y_ref[t, here, :] = y_ref[t, here, :] + out[span, lanes]
                col_ref[t, here, :] = decay[span, lanes]
        return carry, before

    for at, step in ((0, row_block), (ROWS, col_block)):
        end, whole = lax.fori_loop(0, N_SPACE, step, (carry, before))
        state_ref[at : at + STATE_DIM, :] = end
        state_ref[at + STATE_DIM : at + ROWS, :] = jnp.broadcast_to(whole, (8, WIN))


def scan_finish(ids, in_ref, y_ref, row_ref, col_ref, state_ref, gain_ref, out_ref):
    odd = ids[2] % 2
    same = iota((WIN, WIN), 0) // 64 == iota((WIN, WIN), 1) // 64
    same = jnp.where(same, 1.0, 0.0).astype(BF16)
    row_high, row_low = split_high(state_ref[:STATE_DIM, :])
    col_high, col_low = split_high(state_ref[ROWS : ROWS + STATE_DIM, :])
    gain = gain_ref[...]
    for s in range(N_SPACE):
        here = slice(s * TOKENS, (s + 1) * TOKENS)
        c_proj = in_ref[s][:, WIN + STATE_DIM :]
        y, row_decay, col_decay = (
            jnp.concatenate([ref[0, here, :], ref[1, here, :]], axis=1)
            for ref in (y_ref, row_ref, col_ref)
        )
        total = y + row_decay * (dot(c_proj, row_high) + dot(c_proj, row_low))
        total = total + col_decay * (dot(c_proj, col_high) + dot(c_proj, col_low))
        high, low = split_high(total * total)
        meansq = (dot(high, same) + dot(low, same)) * (1.0 / SCAN_DIM)
        normed = total * lax.rsqrt(meansq + EPS) * gain
        left, right = normed[:, :128], normed[:, 128:]
        full = jnp.where(odd == 1, right, left)
        part = jnp.where(odd == 1, left, right)
        out_ref[s, :TOKENS, :] = full.astype(BF16)
        out_ref[s, TOKENS:, :] = (part[:64] + pltpu.roll(part[64:], 64, 1)).astype(BF16)


def join(earlier, later):
    decay = jnp.exp(later[:, STATE_DIM : STATE_DIM + 1, :])
    states = jnp.arange(ROWS)[None, :, None] < STATE_DIM
    return jnp.where(states, decay, 1.0) * earlier + later


def states_before(own, frame):
    total = own
    before = jnp.zeros_like(own)
    for bit in (1, 2, 4, 8, 16):
        other = lax.ppermute(total, "tm", [(i, i ^ bit) for i in range(N_TM)])
        upper = (frame & bit) > 0
        before = jnp.where(upper, join(other, before), before)
        if bit < 16:
            total = jnp.where(upper, join(other, total), join(total, other))
    return before


def add_up(ids, scan_ref, *rest):
    group = ids[0]
    out_ref, total = rest[4], rest[5]
    low_half = iota((64, 128), 1) < 64
    for k in range(4):
        even, uneven = scan_ref[2 * k], scan_ref[2 * k + 1]
        e, o = even[TOKENS:].astype(F32), uneven[TOKENS:].astype(F32)
        total[:, 384 * k : 384 * k + 128] = even[:TOKENS].astype(F32)
        total[:64, 384 * k + 128 : 384 * k + 256] = jnp.where(low_half, e, o)
        total[64:, 384 * k + 128 : 384 * k + 256] = jnp.where(
            low_half, pltpu.roll(e, 64, 1), pltpu.roll(o, 64, 1)
        )
        total[:, 384 * k + 256 : 384 * k + 384] = uneven[:TOKENS].astype(F32)
    for i in range(4):
        cols = pl.ds(pl.multiple_of((group ^ i) * GROUP, 128), GROUP)
        out_ref[:, cols] = (total[:, cols] + rest[i][...].astype(F32)).astype(BF16)


def z_shift(array, by):
    pairs = []
    for half in range(2):
        for z in range(8):
            for core in range(2):
                pairs.append((16 * half + 2 * z + core, 16 * half + 2 * ((z + by) % 8) + core))
    return lax.ppermute(array, "tm", pairs)


def partner(array, bits):
    return lax.ppermute(array, "tm", [(i, i ^ bits) for i in range(N_TM)])


def on_device(queries, keys, values, tile_mask, inner_x, bc_proj, log_decay, col_order, norm_gain):
    frame = lax.axis_index("tm")
    tile = lax.axis_index("space")
    group = 2 * (frame // 16) + frame % 2
    ids = jnp.stack([group, (frame // 2) % 8, tile]).astype(jnp.int32)

    qkv = jax.ShapeDtypeStruct((3, TOKENS, GROUP), BF16)
    own, to_core, to_half, to_both = call(
        head_groups, (qkv,) * 4, 1, 3, moved=4 * 3 * TOKENS * HEADS * HEAD_DIM
    )(ids, queries, keys, values)
    from_core = partner(to_core, 1)
    chunk_a = jnp.stack([own[1:], from_core[1:]])

    sent = call(
        scan_pack, jax.ShapeDtypeStruct((N_SPACE, TOKENS, WIN + 128), BF16), 0, 3, moved=1 << 20
    )(inner_x, bc_proj, log_decay)
    frame_in = lax.all_to_all(sent, "space", split_axis=0, concat_axis=0, tiled=True)

    from_half = partner(to_half, 16)
    from_both = partner(to_both, 17)
    chunk_b = jnp.stack([from_half[1:], from_both[1:]])
    q_all = jnp.stack([own[0], from_core[0], from_half[0], from_both[0]])
    q_all = q_all.reshape(2, 2, TOKENS, GROUP)

    frame_tokens = N_SPACE * TOKENS
    wide = jax.ShapeDtypeStruct((2, frame_tokens, 128), F32)
    y, row_decay, col_decay, state = call(
        scan_frame,
        (wide, wide, wide, jax.ShapeDtypeStruct((2 * ROWS, WIN), F32)),
        2,
        1,
        scratch=[pltpu.VMEM((3, frame_tokens, 128), F32)] * 2,
        flops=1 << 30,
        moved=4 << 20,
    )(ids, col_order, frame_in)

    state = states_before(state.reshape(2, ROWS, WIN), frame).reshape(2 * ROWS, WIN)
    gain = lax.dynamic_slice(norm_gain, (384 * (tile // 2) + 128 * (tile % 2),), (WIN,))
    normed = call(
        scan_finish,
        jax.ShapeDtypeStruct((N_SPACE, 192, 128), BF16),
        1,
        6,
        flops=1 << 29,
        moved=4 << 20,
    )(ids, frame_in, y, row_decay, col_decay, state, gain.reshape(1, WIN))
    scan_rows = lax.all_to_all(normed, "space", split_axis=0, concat_axis=0, tiled=True)

    chunks = {(0, 0): chunk_a, (1, 0): chunk_b}
    flash = call(attend_own, STATE, 2, 3, flops=2 * ITEM_FLOPS, moved=4 << 20)(
        ids, tile_mask, q_all, chunk_a, chunk_b
    )
    for source, step in ((0, 1), (0, 2), (1, 1), (0, 3), (1, 2), (1, 3)):
        for sign in (1, -1):
            behind = chunks[source, sign * (step - 1)]
            chunks[source, sign * step] = z_shift(behind, -sign)
        items = ((source, step, None), (source, -step, None))
        flash = call(
            functools.partial(attend_pair, items), STATE, 2, 6, flops=2 * ITEM_FLOPS, moved=4 << 20
        )(ids, tile_mask, q_all, chunks[source, step], chunks[source, -step], *flash)
    far_a = z_shift(chunks[0, 3], -1)
    far_b = z_shift(chunks[1, -3], 1)
    piece = jax.ShapeDtypeStruct((TOKENS, GROUP), BF16)
    pieces = call(
        attend_last,
        (piece,) * 4,
        2,
        6,
        scratch=[pltpu.VMEM(s.shape, s.dtype) for s in STATE],
        flops=4 * ITEM_FLOPS,
        moved=4 << 20,
    )(ids, tile_mask, q_all, far_a, far_b, *flash)
    attention = (
        pieces[0],
        partner(pieces[1], 1),
        partner(pieces[2], 16),
        partner(pieces[3], 17),
    )
    return call(
        add_up,
        jax.ShapeDtypeStruct((TOKENS, HEADS * HEAD_DIM), BF16),
        1,
        5,
        scratch=[pltpu.VMEM((TOKENS, HEADS * HEAD_DIM), F32)],
        moved=2 << 20,
    )(ids, scan_rows, *attention)


def solution(mesh):
    return jax.shard_map(
        on_device,
        mesh=mesh,
        in_specs=(
            P(("tm", "space"), None),
            P(("tm", "space"), None),
            P(("tm", "space"), None),
            P(),
            P(("tm", "space"), None),
            P(("tm", "space"), None),
            P(None, ("tm", "space")),
            P(),
            P(),
        ),
        out_specs=P(("tm", "space"), None),
        check_vma=False,
    )
```

time: 683 us -> 158 us (0.23)
  the two profiles are of different devices: /device:TPU:8 before, /device:TPU:1 now
where the time goes in v1:
time: 158 us; the launch traced here: 157 us
  starting transfers between devices  58.4 us (37%)
  Pallas kernels  46.3 us (29%)
  waiting for transfers between devices  43 us (27%)
  local copies, waits for them, and re-layouts  8.41 us (5%)
    ppermute x5, waiting for transfers between devices, states_before(): other = lax.ppermute(total, 'tm', [(i, i ^ bit) for i in range(N_TM)])  34.7 us
    ppermute x14, starting transfers between devices, z_shift(): return lax.ppermute(array, 'tm', pairs)  25 us
    pallas_call x6, Pallas kernels, on_device(): call(functools.partial(attend_pair, items), STATE, 2, 6, flops=2 * ITEM_F...  17.6 us
    pallas_call x1, Pallas kernels, on_device(): call(scan_frame, (wide, wide, wide, jax.ShapeDtypeStruct((2 * ROWS, WIN),...  14.3 us
    ppermute x6, starting transfers between devices, partner(): return lax.ppermute(array, 'tm', [(i, i ^ bits) for i in range(N_TM)])  13.9 us
    ppermute x5, starting transfers between devices, states_before(): other = lax.ppermute(total, 'tm', [(i, i ^ bit) for i in range(N_TM)])  12.1 us
    ppermute x6, waiting for transfers between devices, partner(): return lax.ppermute(array, 'tm', [(i, i ^ bits) for i in range(N_TM)])  7.04 us
    pallas_call x1, Pallas kernels, on_device(): call(attend_last, (piece,) * 4, 2, 6, scratch=[pltpu.VMEM(s.shape, s.dtyp...  4.92 us
  transfers between devices with their start and end apart: 27, of which 8 were waited for; matrix products, arithmetic and copies ran while one was open for 3% of the time, Pallas kernels for 28%

profile of v1, /device:TPU:1, one launch (start us, length us, event | category | flops | bytes accessed | tf_op | source)
XLA Modules:
  0.0 157.4 jit_solution(12948611929099617338)
XLA Ops:
  0.1 1.0 copy-done.1
  1.1 1.0 copy-done.2
  2.1 1.0 copy-done.3
  3.7 3.3 %collective-permute-start.5 = (bf16[3,128,384]{2,1,0:T(8,128)(2,1)S(1)}, bf16[3,128,384]{2,1,0:T(8,128)(2,1)S(1)}, u32[]{:S(2)}, u32[]{:S(2)}) collective-permute-start(bf16[3,128,384]{2,1,0:T(8,128)(2,1)S(1)} %get-tuple-element.43), channel_id=1, source_target_pairs={{0,8},{8,0},{16,24},{24,16},{32,40},{40,32},{48,56},{56,48},{64,72... | collective-permute-start | bytes 884744 | tf_op jit(solution)/shard_map/ppermute | solution.py:329
  7.1 1.0 collective-permute-start.6
  8.1 2.2 %collective-permute-start.7 = (bf16[3,128,384]{2,1,0:T(8,128)(2,1)S(1)}, bf16[3,128,384]{2,1,0:T(8,128)(2,1)}, u32[]{:S(2)}, u32[]{:S(2)}) collective-permute-start(bf16[3,128,384]{2,1,0:T(8,128)(2,1)S(1)} %get-tuple-element.45), channel_id=1, source_target_pairs={{0,136},{8,128},{16,152},{24,144},{32,168},{40,160},{48,184},{56,1... | collective-permute-start | bytes 884744 | tf_op jit(solution)/shard_map/ppermute | solution.py:329
  10.3 1.2 shard_map.91
  11.5 3.5 %all-to-all-start = ((bf16[8,128,384]{2,1,0:T(8,128)(2,1)}), bf16[8,128,384]{2,1,0:T(8,128)(2,1)S(1)}, u32[]{:S(2)}, u32[]{:S(2)}) async-start(bf16[8,128,384]{2,1,0:T(8,128)(2,1)} %shard_map.91), calls=%async_computation | async-start | bytes 1572864 | tf_op jit(solution)/shard_map/all_to_all | solution.py:348
  15.7 0.8 dynamic_slice.3
  16.6 1.5 collective-permute-start.19
  18.2 4.0 %collective-permute-start.8 = (bf16[2,2,128,384]{3,2,1,0:T(8,128)(2,1)S(1)}, bf16[2,2,128,384]{3,2,1,0:T(8,128)(2,1)S(1)}, u32[]{:S(2)}, u32[]{:S(2)}) collective-permute-start(bf16[2,2,128,384]{3,2,1,0:T(8,128)(2,1)S(1)} %pad_maximum_fusion.1.a_ref), channel_id=1, source_target_pairs={{0,112},{8,120},{16,0},{24,8},{32,16},{40,24},{48,32},{56,40},{64,... | collective-permute-start | bytes 1179656 | tf_op jit(solution)/shard_map/ppermute | solution.py:325
  22.2 2.0 %collective-permute-done.7 = bf16[3,128,384]{2,1,0:T(8,128)(2,1)} collective-permute-done((bf16[3,128,384]{2,1,0:T(8,128)(2,1)S(1)}, bf16[3,128,384]{2,1,0:T(8,128)(2,1)}, u32[]{:S(2)}, u32[]{:S(2)}) %collective-permute-start.7) | collective-permute-done | bytes 294944 | tf_op jit(solution)/shard_map/ppermute | solution.py:329
  24.2 0.9 slice_bitcast_fusion
  26.0 3.9 %collective-permute-start.16 = (bf16[2,2,128,384]{3,2,1,0:T(8,128)(2,1)S(1)}, bf16[2,2,128,384]{3,2,1,0:T(8,128)(2,1)S(1)}, u32[]{:S(2)}, u32[]{:S(2)}) collective-permute-start(bf16[2,2,128,384]{3,2,1,0:T(8,128)(2,1)S(1)} %pad_maximum_fusion.2.b_ref), channel_id=1, source_target_pairs={{0,112},{8,120},{16,0},{24,8},{32,16},{40,24},{48,32},{56,40},{64,... | collective-permute-start | bytes 1179656 | tf_op jit(solution)/shard_map/ppermute | solution.py:325
  29.9 1.6 slice.94
  31.5 1.2 all-to-all-done.in_ref
  32.7 14.3 %shard_map.92 = (f32[2,1024,128]{2,1,0:T(8,128)S(1)}, f32[2,1024,128]{2,1,0:T(8,128)S(1)}, f32[2,1024,128]{2,1,0:T(8,128)S(1)}, f32[144,256]{1,0:T(8,128)S(1)}) custom-call(s32[3]{0:T(128)S(1)} %pad_add_fusion.ids, s32[32]{0:T(128)S(1)} %copy-done.9, bf16[8,128,384]{2,1,0:T(8,128)(2,1)S(1)} %all-to-all-done.in_ref), custom_call_target="tpu_custom_call" | custom-call | flops 1073741824 | bytes 4194304 | tf_op jit(solution)/shard_map/pallas_call | solution.py:358
  47.0 1.0 collective-permute-start
  48.0 1.7 %collective-permute-start.20 = (bf16[2,2,128,384]{3,2,1,0:T(8,128)(2,1)S(1)}, bf16[2,2,128,384]{3,2,1,0:T(8,128)(2,1)}, u32[]{:S(2)}, u32[]{:S(2)}) collective-permute-start(bf16[2,2,128,384]{3,2,1,0:T(8,128)(2,1)S(1)} %collective-permute-done.19.c1), channel_id=1, source_target_pairs={{0,16},{8,24},{16,32},{24,40},{32,48},{40,56},{48,64},{56,72},{64,... | collective-permute-start | bytes 1179656 | tf_op jit(solution)/shard_map/ppermute | solution.py:325
  49.7 4.0 %collective-permute-start.9 = (bf16[2,2,128,384]{3,2,1,0:T(8,128)(2,1)S(1)}, bf16[2,2,128,384]{3,2,1,0:T(8,128)(2,1)S(1)}, u32[]{:S(2)}, u32[]{:S(2)}) collective-permute-start(bf16[2,2,128,384]{3,2,1,0:T(8,128)(2,1)S(1)} %collective-permute-done.8.c0), channel_id=1, source_target_pairs={{0,112},{8,120},{16,0},{24,8},{32,16},{40,24},{48,32},{56,40},{64,... | collective-permute-start | bytes 1179656 | tf_op jit(solution)/shard_map/ppermute | solution.py:325
  53.7 2.7 %collective-permute-start.17 = (bf16[2,2,128,384]{3,2,1,0:T(8,128)(2,1)S(1)}, bf16[2,2,128,384]{3,2,1,0:T(8,128)(2,1)}, u32[]{:S(2)}, u32[]{:S(2)}) collective-permute-start(bf16[2,2,128,384]{3,2,1,0:T(8,128)(2,1)S(1)} %collective-permute-done.16.c0), channel_id=1, source_target_pairs={{0,112},{8,120},{16,0},{24,8},{32,16},{40,24},{48,32},{56,40},{64,... | collective-permute-start | bytes 1179656 | tf_op jit(solution)/shard_map/ppermute | solution.py:325
  56.7 15.4 %collective-permute-done.1 = f32[2,72,256]{2,1,0:T(8,128)S(1)} collective-permute-done((f32[2,72,256]{2,1,0:T(8,128)S(1)}, f32[2,72,256]{2,1,0:T(8,128)S(1)}, u32[]{:S(2)}, u32[]{:S(2)}) %collective-permute-start.1) | collective-permute-done | bytes 147488 | tf_op jit(solution)/shard_map/ppermute | solution.py:293
  72.2 4.4 %collective-permute-start.2 = (f32[2,72,256]{2,1,0:T(8,128)S(1)}, f32[2,72,256]{2,1,0:T(8,128)S(1)}, u32[]{:S(2)}, u32[]{:S(2)}) collective-permute-start(f32[2,72,256]{2,1,0:T(8,128)S(1)} %get-tuple-element.75), channel_id=1, source_target_pairs={{0,32},{8,40},{16,48},{24,56},{32,0},{40,8},{48,16},{56,24},{64,96... | collective-permute-start | bytes 442376 | tf_op jit(solution)/shard_map/ppermute | solution.py:293
  76.7 0.8 collective-permute-start.10
  78.3 2.6 %collective-permute-start.18 = (bf16[2,2,128,384]{3,2,1,0:T(8,128)(2,1)}, bf16[2,2,128,384]{3,2,1,0:T(8,128)(2,1)}, u32[]{:S(2)}, u32[]{:S(2)}) collective-permute-start(bf16[2,2,128,384]{3,2,1,0:T(8,128)(2,1)} %collective-permute-done.17.c0), channel_id=1, source_target_pairs={{0,112},{8,120},{16,0},{24,8},{32,16},{40,24},{48,32},{56,40},{64,... | collective-permute-start | bytes 1179656 | tf_op jit(solution)/shard_map/ppermute | solution.py:325
  80.9 2.2 %collective-permute-done.2 = f32[2,72,256]{2,1,0:T(8,128)S(1)} collective-permute-done((f32[2,72,256]{2,1,0:T(8,128)S(1)}, f32[2,72,256]{2,1,0:T(8,128)S(1)}, u32[]{:S(2)}, u32[]{:S(2)}) %collective-permute-start.2) | collective-permute-done | bytes 147488 | tf_op jit(solution)/shard_map/ppermute | solution.py:293
  83.3 4.8 %collective-permute-start.3 = (f32[2,72,256]{2,1,0:T(8,128)S(1)}, f32[2,72,256]{2,1,0:T(8,128)S(1)}, u32[]{:S(2)}, u32[]{:S(2)}) collective-permute-start(f32[2,72,256]{2,1,0:T(8,128)S(1)} %get-tuple-element.73), channel_id=1, source_target_pairs={{0,64},{8,72},{16,80},{24,88},{32,96},{40,104},{48,112},{56,120},{... | collective-permute-start | bytes 442376 | tf_op jit(solution)/shard_map/ppermute | solution.py:293
  88.2 16.2 %collective-permute-done.3 = f32[2,72,256]{2,1,0:T(8,128)S(1)} collective-permute-done((f32[2,72,256]{2,1,0:T(8,128)S(1)}, f32[2,72,256]{2,1,0:T(8,128)S(1)}, u32[]{:S(2)}, u32[]{:S(2)}) %collective-permute-start.3) | collective-permute-done | bytes 147488 | tf_op jit(solution)/shard_map/ppermute | solution.py:293
  104.5 1.8 %collective-permute-start.4 = (f32[2,72,256]{2,1,0:T(8,128)S(1)}, f32[2,72,256]{2,1,0:T(8,128)S(1)}, u32[]{:S(2)}, u32[]{:S(2)}) collective-permute-start(f32[2,72,256]{2,1,0:T(8,128)S(1)} %get-tuple-element.71), channel_id=1, source_target_pairs={{0,128},{8,136},{16,144},{24,152},{32,160},{40,168},{48,176},{56,1... | collective-permute-start | bytes 442376 | tf_op jit(solution)/shard_map/ppermute | solution.py:293
  106.4 1.8 %collective-permute-start.15 = (bf16[2,2,128,384]{3,2,1,0:T(8,128)(2,1)}, bf16[2,2,128,384]{3,2,1,0:T(8,128)(2,1)}, u32[]{:S(2)}, u32[]{:S(2)}) collective-permute-start(bf16[2,2,128,384]{3,2,1,0:T(8,128)(2,1)} %collective-permute-done.14.c1), channel_id=1, source_target_pairs={{0,16},{8,24},{16,32},{24,40},{32,48},{40,56},{48,64},{56,72},{64,... | collective-permute-start | bytes 1179656 | tf_op jit(solution)/shard_map/ppermute | solution.py:325
  108.1 1.0 collective-permute-start.11
  109.1 1.0 collective-permute-done.4
  110.2 3.4 %shard_map.93 = bf16[8,192,128]{2,1,0:T(8,128)(2,1)} custom-call(s32[3]{0:T(128)S(1)} %pad_add_fusion.ids, bf16[8,128,384]{2,1,0:T(8,128)(2,1)S(1)} %all-to-all-done.in_ref, f32[2,1024,128]{2,1,0:T(8,128)S(1)} %get-tuple-element.38.y_ref, f32[2,1024,128]{2,1,0:T(8,128)S(1)} %get-tuple-element.39.row_ref, f32[2,1024,128]{2,1,0:T(8,128)S(1)} %get-tuple-element.40.col_ref, ...), custom_call_target="tpu_custom_call" | custom-call | flops 536870912 | bytes 4194304 | tf_op jit(solution)/shard_map/pallas_call | solution.py:370
  113.6 3.8 %all-to-all-start.1 = ((bf16[8,192,128]{2,1,0:T(8,128)(2,1)}), bf16[8,192,128]{2,1,0:T(8,128)(2,1)S(1)}, u32[]{:S(2)}, u32[]{:S(2)}) async-start(bf16[8,192,128]{2,1,0:T(8,128)(2,1)} %shard_map.93), calls=%async_computation.1 | async-start | bytes 786432 | tf_op jit(solution)/shard_map/all_to_all | solution.py:378
  118.2 2.7 %shard_map.95 = (f32[2,8,256]{2,1,0:T(8,128)S(1)}, f32[2,8,256]{2,1,0:T(8,128)S(1)}, f32[2,3,128,256]{3,2,1,0:T(8,128)S(1)}) custom-call(s32[3]{0:T(128)S(1)} %pad_add_fusion.ids, s32[32,32]{1,0:T(8,128)S(1)} %copy-done, bf16[2,2,128,384]{3,2,1,0:T(8,128)(2,1)S(1)} %bitcast.51, bf16[2,2,128,384]{3,2,1,0:T(8,128)(2,1)S(1)} %pad_maximum_fusion.1.a_ref, ...), custom_call_target="tpu_custom_call" | custom-call | flops 201326592 | bytes 4194304 | tf_op jit(solution)/shard_map/pallas_call | solution.py:381
  120.9 2.8 %shard_map.96 = (f32[2,8,256]{2,1,0:T(8,128)S(1)}, f32[2,8,256]{2,1,0:T(8,128)S(1)}, f32[2,3,128,256]{3,2,1,0:T(8,128)S(1)}) custom-call(s32[3]{0:T(128)S(1)} %pad_add_fusion.ids, s32[32,32]{1,0:T(8,128)S(1)} %copy-done, bf16[2,2,128,384]{3,2,1,0:T(8,128)(2,1)S(1)} %bitcast.52, bf16[2,2,128,384]{3,2,1,0:T(8,128)(2,1)S(1)} %collective-permute-done.8.c0, ...), custom_call_target="tpu_custom_call" | custom-call | flops 201326592 | bytes 4194304 | tf_op jit(solution)/shard_map/pallas_call | solution.py:389
  123.7 3.0 %shard_map.97 = (f32[2,8,256]{2,1,0:T(8,128)S(1)}, f32[2,8,256]{2,1,0:T(8,128)S(1)}, f32[2,3,128,256]{3,2,1,0:T(8,128)S(1)}) custom-call(s32[3]{0:T(128)S(1)} %pad_add_fusion.ids, s32[32,32]{1,0:T(8,128)S(1)} %copy-done, bf16[2,2,128,384]{3,2,1,0:T(8,128)(2,1)S(1)} %bitcast.53, bf16[2,2,128,384]{3,2,1,0:T(8,128)(2,1)S(1)} %copy-done.6, ...), custom_call_target="tpu_custom_call" | custom-call | flops 201326592 | bytes 4194304 | tf_op jit(solution)/shard_map/pallas_call | solution.py:389
  126.7 2.8 %shard_map.98 = (f32[2,8,256]{2,1,0:T(8,128)S(1)}, f32[2,8,256]{2,1,0:T(8,128)S(1)}, f32[2,3,128,256]{3,2,1,0:T(8,128)S(1)}) custom-call(s32[3]{0:T(128)S(1)} %pad_add_fusion.ids, s32[32,32]{1,0:T(8,128)S(1)} %copy-done, bf16[2,2,128,384]{3,2,1,0:T(8,128)(2,1)S(1)} %bitcast.54, bf16[2,2,128,384]{3,2,1,0:T(8,128)(2,1)S(1)} %collective-permute-done.16.c0, ...), custom_call_target="tpu_custom_call" | custom-call | flops 201326592 | bytes 4194304 | tf_op jit(solution)/shard_map/pallas_call | solution.py:389
  129.5 3.1 %shard_map.99 = (f32[2,8,256]{2,1,0:T(8,128)S(1)}, f32[2,8,256]{2,1,0:T(8,128)S(1)}, f32[2,3,128,256]{3,2,1,0:T(8,128)S(1)}) custom-call(s32[3]{0:T(128)S(1)} %pad_add_fusion.ids, s32[32,32]{1,0:T(8,128)S(1)} %copy-done, bf16[2,2,128,384]{3,2,1,0:T(8,128)(2,1)S(1)} %bitcast.55, bf16[2,2,128,384]{3,2,1,0:T(8,128)(2,1)} %collective-permute-done.10.c0, ...), custom_call_target="tpu_custom_call" | custom-call | flops 201326592 | bytes 4194304 | tf_op jit(solution)/shard_map/pallas_call | solution.py:389
  132.6 3.0 %shard_map.100 = (f32[2,8,256]{2,1,0:T(8,128)S(1)}, f32[2,8,256]{2,1,0:T(8,128)S(1)}, f32[2,3,128,256]{3,2,1,0:T(8,128)S(1)}) custom-call(s32[3]{0:T(128)S(1)} %pad_add_fusion.ids, s32[32,32]{1,0:T(8,128)S(1)} %copy-done, bf16[2,2,128,384]{3,2,1,0:T(8,128)(2,1)S(1)} %bitcast.56, bf16[2,2,128,384]{3,2,1,0:T(8,128)(2,1)} %collective-permute-done.17.c0, ...), custom_call_target="tpu_custom_call" | custom-call | flops 201326592 | bytes 4194304 | tf_op jit(solution)/shard_map/pallas_call | solution.py:389
  135.5 3.1 %shard_map.101 = (f32[2,8,256]{2,1,0:T(8,128)S(1)}, f32[2,8,256]{2,1,0:T(8,128)S(1)}, f32[2,3,128,256]{3,2,1,0:T(8,128)S(1)}) custom-call(s32[3]{0:T(128)S(1)} %pad_add_fusion.ids, s32[32,32]{1,0:T(8,128)S(1)} %copy-done, bf16[2,2,128,384]{3,2,1,0:T(8,128)(2,1)S(1)} %bitcast.57, bf16[2,2,128,384]{3,2,1,0:T(8,128)(2,1)} %collective-permute-done.18.c0, ...), custom_call_target="tpu_custom_call" | custom-call | flops 201326592 | bytes 4194304 | tf_op jit(solution)/shard_map/pallas_call | solution.py:389
  138.7 4.9 %shard_map.102 = (bf16[128,384]{1,0:T(8,128)(2,1)S(1)}, bf16[128,384]{1,0:T(8,128)(2,1)S(1)}, bf16[128,384]{1,0:T(8,128)(2,1)S(1)}, bf16[128,384]{1,0:T(8,128)(2,1)S(1)}) custom-call(s32[3]{0:T(128)S(1)} %pad_add_fusion.ids, s32[32,32]{1,0:T(8,128)S(1)} %copy-done, bf16[2,2,128,384]{3,2,1,0:T(8,128)(2,1)S(1)} %bitcast.58, ...), custom_call_target="tpu_custom_call" | custom-call | flops 402653184 | bytes 4194304 | tf_op jit(solution)/shard_map/pallas_call | solution.py:395
  143.6 4.1 %collective-permute-start.22 = (bf16[128,384]{1,0:T(8,128)(2,1)S(1)}, bf16[128,384]{1,0:T(8,128)(2,1)S(1)}, u32[]{:S(2)}, u32[]{:S(2)}) collective-permute-start(bf16[128,384]{1,0:T(8,128)(2,1)S(1)} %get-tuple-element.68), channel_id=1, source_target_pairs={{0,8},{8,0},{16,24},{24,16},{32,40},{40,32},{48,56},{56,48},{64,72... | collective-permute-start | bytes 294920 | tf_op jit(solution)/shard_map/ppermute | solution.py:329
  147.7 1.7 %collective-permute-start.23 = (bf16[128,384]{1,0:T(8,128)(2,1)S(1)}, bf16[128,384]{1,0:T(8,128)(2,1)S(1)}, u32[]{:S(2)}, u32[]{:S(2)}) collective-permute-start(bf16[128,384]{1,0:T(8,128)(2,1)S(1)} %get-tuple-element.69), channel_id=1, source_target_pairs={{0,128},{8,136},{16,144},{24,152},{32,160},{40,168},{48,176},{56,1... | collective-permute-start | bytes 294920 | tf_op jit(solution)/shard_map/ppermute | solution.py:329
  149.4 1.5 collective-permute-start.24
  150.9 2.6 %collective-permute-done.23.rest_2_ = bf16[128,384]{1,0:T(8,128)(2,1)S(1)} collective-permute-done((bf16[128,384]{1,0:T(8,128)(2,1)S(1)}, bf16[128,384]{1,0:T(8,128)(2,1)S(1)}, u32[]{:S(2)}, u32[]{:S(2)}) %collective-permute-start.23) | collective-permute-done | bytes 98336 | tf_op jit(solution)/shard_map/ppermute | solution.py:329
  153.5 2.4 %collective-permute-done.24.rest_3_ = bf16[128,384]{1,0:T(8,128)(2,1)S(1)} collective-permute-done((bf16[128,384]{1,0:T(8,128)(2,1)S(1)}, bf16[128,384]{1,0:T(8,128)(2,1)S(1)}, u32[]{:S(2)}, u32[]{:S(2)}) %collective-permute-start.24) | collective-permute-done | bytes 98336 | tf_op jit(solution)/shard_map/ppermute | solution.py:329
  155.9 1.5 shard_map.103
  (91 shorter events, 4.7 us)
Async XLA Ops:
  0.1 1.0 copy-start.1
  1.1 1.0 copy-start.2
  2.1 1.0 copy-start.3
  3.1 7.2 %copy-start.4 = (bf16[128,1536]{1,0:T(8,128)(2,1)S(1)}, bf16[128,1536]{1,0:T(8,128)(2,1)}, u32[]{:S(2)}) copy-start(bf16[128,1536]{1,0:T(8,128)(2,1)} %x_ref.1) | copy-start | bytes 1179652
  3.1 7.2 %copy-start.7 = (bf16[128,128]{1,0:T(8,128)(2,1)S(1)}, bf16[128,128]{1,0:T(8,128)(2,1)}, u32[]{:S(2)}) copy-start(bf16[128,128]{1,0:T(8,128)(2,1)} %bc_ref.1) | copy-start | bytes 98308
  3.1 7.2 %copy-start.8 = (bf16[24,128]{1,0:T(8,128)(2,1)S(1)}, bf16[24,128]{1,0:T(8,128)(2,1)}, u32[]{:S(2)}) copy-start(bf16[24,128]{1,0:T(8,128)(2,1)} %log_ref.1) | copy-start | bytes 18436
  3.7 12.8 %collective-permute-start.5 = (bf16[3,128,384]{2,1,0:T(8,128)(2,1)S(1)}, bf16[3,128,384]{2,1,0:T(8,128)(2,1)S(1)}, u32[]{:S(2)}, u32[]{:S(2)}) collective-permute-start(bf16[3,128,384]{2,1,0:T(8,128)(2,1)S(1)} %get-tuple-element.43), channel_id=1, source_target_pairs={{0,8},{8,0},{16,24},{24,16},{32,40},{40,32},{48,56},{56,48},{64,72... | collective-permute-start | bytes 884744 | tf_op jit(solution)/shard_map/ppermute | solution.py:329
  7.1 18.1 %collective-permute-start.6 = (bf16[3,128,384]{2,1,0:T(8,128)(2,1)S(1)}, bf16[3,128,384]{2,1,0:T(8,128)(2,1)S(1)}, u32[]{:S(2)}, u32[]{:S(2)}) collective-permute-start(bf16[3,128,384]{2,1,0:T(8,128)(2,1)S(1)} %get-tuple-element.44), channel_id=1, source_target_pairs={{0,128},{8,136},{16,144},{24,152},{32,160},{40,168},{48,176},{56,1... | collective-permute-start | bytes 884744 | tf_op jit(solution)/shard_map/ppermute | solution.py:329
  8.1 16.1 %collective-permute-start.7 = (bf16[3,128,384]{2,1,0:T(8,128)(2,1)S(1)}, bf16[3,128,384]{2,1,0:T(8,128)(2,1)}, u32[]{:S(2)}, u32[]{:S(2)}) collective-permute-start(bf16[3,128,384]{2,1,0:T(8,128)(2,1)S(1)} %get-tuple-element.45), channel_id=1, source_target_pairs={{0,136},{8,128},{16,152},{24,144},{32,168},{40,160},{48,184},{56,1... | collective-permute-start | bytes 884744 | tf_op jit(solution)/shard_map/ppermute | solution.py:329
  11.5 21.2 %all-to-all-start = ((bf16[8,128,384]{2,1,0:T(8,128)(2,1)}), bf16[8,128,384]{2,1,0:T(8,128)(2,1)S(1)}, u32[]{:S(2)}, u32[]{:S(2)}) async-start(bf16[8,128,384]{2,1,0:T(8,128)(2,1)} %shard_map.91), calls=%async_computation | async-start | bytes 1572864 | tf_op jit(solution)/shard_map/all_to_all | solution.py:348
  16.5 13.4 %copy-start.11 = (bf16[3,128,384]{2,1,0:T(8,128)(2,1)}, bf16[3,128,384]{2,1,0:T(8,128)(2,1)S(1)}, u32[]{:S(2)}) copy-start(bf16[3,128,384]{2,1,0:T(8,128)(2,1)S(1)} %collective-permute-done.5) | copy-start | bytes 884740
  16.6 31.4 %collective-permute-start.19 = (bf16[2,2,128,384]{3,2,1,0:T(8,128)(2,1)S(1)}, bf16[2,2,128,384]{3,2,1,0:T(8,128)(2,1)S(1)}, u32[]{:S(2)}, u32[]{:S(2)}) collective-permute-start(bf16[2,2,128,384]{3,2,1,0:T(8,128)(2,1)S(1)} %pad_maximum_fusion.1.a_ref), channel_id=1, source_target_pairs={{0,16},{8,24},{16,32},{24,40},{32,48},{40,56},{48,64},{56,72},{64,... | collective-permute-start | bytes 1179656 | tf_op jit(solution)/shard_map/ppermute | solution.py:325
  18.2 31.6 %collective-permute-start.8 = (bf16[2,2,128,384]{3,2,1,0:T(8,128)(2,1)S(1)}, bf16[2,2,128,384]{3,2,1,0:T(8,128)(2,1)S(1)}, u32[]{:S(2)}, u32[]{:S(2)}) collective-permute-start(bf16[2,2,128,384]{3,2,1,0:T(8,128)(2,1)S(1)} %pad_maximum_fusion.1.a_ref), channel_id=1, source_target_pairs={{0,112},{8,120},{16,0},{24,8},{32,16},{40,24},{48,32},{56,40},{64,... | collective-permute-start | bytes 1179656 | tf_op jit(solution)/shard_map/ppermute | solution.py:325
  25.2 0.7 copy-start.12
  25.9 27.8 %collective-permute-start.12 = (bf16[2,2,128,384]{3,2,1,0:T(8,128)(2,1)S(1)}, bf16[2,2,128,384]{3,2,1,0:T(8,128)(2,1)S(1)}, u32[]{:S(2)}, u32[]{:S(2)}) collective-permute-start(bf16[2,2,128,384]{3,2,1,0:T(8,128)(2,1)S(1)} %pad_maximum_fusion.2.b_ref), channel_id=1, source_target_pairs={{0,16},{8,24},{16,32},{24,40},{32,48},{40,56},{48,64},{56,72},{64,... | collective-permute-start | bytes 1179656 | tf_op jit(solution)/shard_map/ppermute | solution.py:325
  26.0 27.8 %collective-permute-start.16 = (bf16[2,2,128,384]{3,2,1,0:T(8,128)(2,1)S(1)}, bf16[2,2,128,384]{3,2,1,0:T(8,128)(2,1)S(1)}, u32[]{:S(2)}, u32[]{:S(2)}) collective-permute-start(bf16[2,2,128,384]{3,2,1,0:T(8,128)(2,1)S(1)} %pad_maximum_fusion.2.b_ref), channel_id=1, source_target_pairs={{0,112},{8,120},{16,0},{24,8},{32,16},{40,24},{48,32},{56,40},{64,... | collective-permute-start | bytes 1179656 | tf_op jit(solution)/shard_map/ppermute | solution.py:325
  29.9 2.7 %copy-start.9 = (s32[32]{0:T(128)S(1)}, s32[32]{0:T(128)}, u32[]{:S(2)}) copy-start(s32[32]{0:T(128)} %order_ref.1) | copy-start | bytes 388
  47.0 9.4 %collective-permute-start = (f32[2,72,256]{2,1,0:T(8,128)S(1)}, f32[2,72,256]{2,1,0:T(8,128)S(1)}, u32[]{:S(2)}, u32[]{:S(2)}) collective-permute-start(f32[2,72,256]{2,1,0:T(8,128)S(1)} %bitcast.60), channel_id=1, source_target_pairs={{0,8},{8,0},{16,24},{24,16},{32,40},{40,32},{48,56},{56,48},{64,72... | collective-permute-start | bytes 442376 | tf_op jit(solution)/shard_map/ppermute | solution.py:293
  48.0 29.5 %collective-permute-start.20 = (bf16[2,2,128,384]{3,2,1,0:T(8,128)(2,1)S(1)}, bf16[2,2,128,384]{3,2,1,0:T(8,128)(2,1)}, u32[]{:S(2)}, u32[]{:S(2)}) collective-permute-start(bf16[2,2,128,384]{3,2,1,0:T(8,128)(2,1)S(1)} %collective-permute-done.19.c1), channel_id=1, source_target_pairs={{0,16},{8,24},{16,32},{24,40},{32,48},{40,56},{48,64},{56,72},{64,... | collective-permute-start | bytes 1179656 | tf_op jit(solution)/shard_map/ppermute | solution.py:325
  49.7 27.0 %collective-permute-start.9 = (bf16[2,2,128,384]{3,2,1,0:T(8,128)(2,1)S(1)}, bf16[2,2,128,384]{3,2,1,0:T(8,128)(2,1)S(1)}, u32[]{:S(2)}, u32[]{:S(2)}) collective-permute-start(bf16[2,2,128,384]{3,2,1,0:T(8,128)(2,1)S(1)} %collective-permute-done.8.c0), channel_id=1, source_target_pairs={{0,112},{8,120},{16,0},{24,8},{32,16},{40,24},{48,32},{56,40},{64,... | collective-permute-start | bytes 1179656 | tf_op jit(solution)/shard_map/ppermute | solution.py:325
  53.7 24.5 %collective-permute-start.13 = (bf16[2,2,128,384]{3,2,1,0:T(8,128)(2,1)S(1)}, bf16[2,2,128,384]{3,2,1,0:T(8,128)(2,1)S(1)}, u32[]{:S(2)}, u32[]{:S(2)}) collective-permute-start(bf16[2,2,128,384]{3,2,1,0:T(8,128)(2,1)S(1)} %collective-permute-done.12.c1), channel_id=1, source_target_pairs={{0,16},{8,24},{16,32},{24,40},{32,48},{40,56},{48,64},{56,72},{64,... | collective-permute-start | bytes 1179656 | tf_op jit(solution)/shard_map/ppermute | solution.py:325
  53.7 24.6 %collective-permute-start.17 = (bf16[2,2,128,384]{3,2,1,0:T(8,128)(2,1)S(1)}, bf16[2,2,128,384]{3,2,1,0:T(8,128)(2,1)}, u32[]{:S(2)}, u32[]{:S(2)}) collective-permute-start(bf16[2,2,128,384]{3,2,1,0:T(8,128)(2,1)S(1)} %collective-permute-done.16.c0), channel_id=1, source_target_pairs={{0,112},{8,120},{16,0},{24,8},{32,16},{40,24},{48,32},{56,40},{64,... | collective-permute-start | bytes 1179656 | tf_op jit(solution)/shard_map/ppermute | solution.py:325
  56.6 15.5 %collective-permute-start.1 = (f32[2,72,256]{2,1,0:T(8,128)S(1)}, f32[2,72,256]{2,1,0:T(8,128)S(1)}, u32[]{:S(2)}, u32[]{:S(2)}) collective-permute-start(f32[2,72,256]{2,1,0:T(8,128)S(1)} %get-tuple-element.77), channel_id=1, source_target_pairs={{0,16},{8,24},{16,0},{24,8},{32,48},{40,56},{48,32},{56,40},{64,80... | collective-permute-start | bytes 442376 | tf_op jit(solution)/shard_map/ppermute | solution.py:293
  72.2 10.9 %collective-permute-start.2 = (f32[2,72,256]{2,1,0:T(8,128)S(1)}, f32[2,72,256]{2,1,0:T(8,128)S(1)}, u32[]{:S(2)}, u32[]{:S(2)}) collective-permute-start(f32[2,72,256]{2,1,0:T(8,128)S(1)} %get-tuple-element.75), channel_id=1, source_target_pairs={{0,32},{8,40},{16,48},{24,56},{32,0},{40,8},{48,16},{56,24},{64,96... | collective-permute-start | bytes 442376 | tf_op jit(solution)/shard_map/ppermute | solution.py:293
  76.7 27.7 %copy-start.5 = (bf16[2,2,128,384]{3,2,1,0:T(8,128)(2,1)}, bf16[2,2,128,384]{3,2,1,0:T(8,128)(2,1)S(1)}, u32[]{:S(2)}) copy-start(bf16[2,2,128,384]{3,2,1,0:T(8,128)(2,1)S(1)} %collective-permute-done.9.c0) | copy-start | bytes 1179652
  76.7 31.4 %collective-permute-start.10 = (bf16[2,2,128,384]{3,2,1,0:T(8,128)(2,1)S(1)}, bf16[2,2,128,384]{3,2,1,0:T(8,128)(2,1)}, u32[]{:S(2)}, u32[]{:S(2)}) collective-permute-start(bf16[2,2,128,384]{3,2,1,0:T(8,128)(2,1)S(1)} %collective-permute-done.9.c0), channel_id=1, source_target_pairs={{0,112},{8,120},{16,0},{24,8},{32,16},{40,24},{48,32},{56,40},{64,... | collective-permute-start | bytes 1179656 | tf_op jit(solution)/shard_map/ppermute | solution.py:325
  77.5 52.0 %collective-permute-start.21 = (bf16[2,2,128,384]{3,2,1,0:T(8,128)(2,1)}, bf16[2,2,128,384]{3,2,1,0:T(8,128)(2,1)}, u32[]{:S(2)}, u32[]{:S(2)}) collective-permute-start(bf16[2,2,128,384]{3,2,1,0:T(8,128)(2,1)} %collective-permute-done.20.c1), channel_id=1, source_target_pairs={{0,16},{8,24},{16,32},{24,40},{32,48},{40,56},{48,64},{56,72},{64,... | collective-permute-start | bytes 1179656 | tf_op jit(solution)/shard_map/ppermute | solution.py:325
  78.2 28.1 %collective-permute-start.14 = (bf16[2,2,128,384]{3,2,1,0:T(8,128)(2,1)S(1)}, bf16[2,2,128,384]{3,2,1,0:T(8,128)(2,1)}, u32[]{:S(2)}, u32[]{:S(2)}) collective-permute-start(bf16[2,2,128,384]{3,2,1,0:T(8,128)(2,1)S(1)} %collective-permute-done.13.c1), channel_id=1, source_target_pairs={{0,16},{8,24},{16,32},{24,40},{32,48},{40,56},{48,64},{56,72},{64,... | collective-permute-start | bytes 1179656 | tf_op jit(solution)/shard_map/ppermute | solution.py:325
  78.3 57.2 %collective-permute-start.18 = (bf16[2,2,128,384]{3,2,1,0:T(8,128)(2,1)}, bf16[2,2,128,384]{3,2,1,0:T(8,128)(2,1)}, u32[]{:S(2)}, u32[]{:S(2)}) collective-permute-start(bf16[2,2,128,384]{3,2,1,0:T(8,128)(2,1)} %collective-permute-done.17.c0), channel_id=1, source_target_pairs={{0,112},{8,120},{16,0},{24,8},{32,16},{40,24},{48,32},{56,40},{64,... | collective-permute-start | bytes 1179656 | tf_op jit(solution)/shard_map/ppermute | solution.py:325
  83.3 21.1 %collective-permute-start.3 = (f32[2,72,256]{2,1,0:T(8,128)S(1)}, f32[2,72,256]{2,1,0:T(8,128)S(1)}, u32[]{:S(2)}, u32[]{:S(2)}) collective-permute-start(f32[2,72,256]{2,1,0:T(8,128)S(1)} %get-tuple-element.73), channel_id=1, source_target_pairs={{0,64},{8,72},{16,80},{24,88},{32,96},{40,104},{48,112},{56,120},{... | collective-permute-start | bytes 442376 | tf_op jit(solution)/shard_map/ppermute | solution.py:293
  104.5 5.6 %collective-permute-start.4 = (f32[2,72,256]{2,1,0:T(8,128)S(1)}, f32[2,72,256]{2,1,0:T(8,128)S(1)}, u32[]{:S(2)}, u32[]{:S(2)}) collective-permute-start(f32[2,72,256]{2,1,0:T(8,128)S(1)} %get-tuple-element.71), channel_id=1, source_target_pairs={{0,128},{8,136},{16,144},{24,152},{32,160},{40,168},{48,176},{56,1... | collective-permute-start | bytes 442376 | tf_op jit(solution)/shard_map/ppermute | solution.py:293
  106.4 32.3 %collective-permute-start.15 = (bf16[2,2,128,384]{3,2,1,0:T(8,128)(2,1)}, bf16[2,2,128,384]{3,2,1,0:T(8,128)(2,1)}, u32[]{:S(2)}, u32[]{:S(2)}) collective-permute-start(bf16[2,2,128,384]{3,2,1,0:T(8,128)(2,1)} %collective-permute-done.14.c1), channel_id=1, source_target_pairs={{0,16},{8,24},{16,32},{24,40},{32,48},{40,56},{48,64},{56,72},{64,... | collective-permute-start | bytes 1179656 | tf_op jit(solution)/shard_map/ppermute | solution.py:325
  108.1 30.5 %collective-permute-start.11 = (bf16[2,2,128,384]{3,2,1,0:T(8,128)(2,1)}, bf16[2,2,128,384]{3,2,1,0:T(8,128)(2,1)}, u32[]{:S(2)}, u32[]{:S(2)}) collective-permute-start(bf16[2,2,128,384]{3,2,1,0:T(8,128)(2,1)} %collective-permute-done.10.c0), channel_id=1, source_target_pairs={{0,112},{8,120},{16,0},{24,8},{32,16},{40,24},{48,32},{56,40},{64,... | collective-permute-start | bytes 1179656 | tf_op jit(solution)/shard_map/ppermute | solution.py:325
  113.6 3.8 %copy-start.10 = (bf16[1,128,384]{2,1,0:T(8,128)(2,1)S(1)}, bf16[1,128,384]{2,1,0:T(8,128)(2,1)}, u32[]{:S(2)}) copy-start(bf16[1,128,384]{2,1,0:T(8,128)(2,1)} %slice.72) | copy-start | bytes 294916
  113.6 3.8 %slice-start = ((bf16[3,128,384]{2,1,0:T(8,128)(2,1)}), bf16[1,128,384]{2,1,0:T(8,128)(2,1)S(1)}, s32[]{:S(2)}) async-start(bf16[3,128,384]{2,1,0:T(8,128)(2,1)} %copy-done.11), calls=%async_computation.2 | async-start | bytes 196608 | tf_op jit(solution)/shard_map/slice | solution.py:353
  113.6 3.9 %slice-start.1 = ((bf16[3,128,384]{2,1,0:T(8,128)(2,1)}), bf16[1,128,384]{2,1,0:T(8,128)(2,1)S(1)}, s32[]{:S(2)}) async-start(bf16[3,128,384]{2,1,0:T(8,128)(2,1)} %copy-done.12), calls=%async_computation.3 | async-start | bytes 196608 | tf_op jit(solution)/shard_map/slice | solution.py:353
  113.6 3.9 %copy-start.13 = (bf16[1,128,384]{2,1,0:T(8,128)(2,1)S(1)}, bf16[1,128,384]{2,1,0:T(8,128)(2,1)}, u32[]{:S(2)}) copy-start(bf16[1,128,384]{2,1,0:T(8,128)(2,1)} %slice.94) | copy-start | bytes 294916
  113.6 37.3 %all-to-all-start.1 = ((bf16[8,192,128]{2,1,0:T(8,128)(2,1)}), bf16[8,192,128]{2,1,0:T(8,128)(2,1)S(1)}, u32[]{:S(2)}, u32[]{:S(2)}) async-start(bf16[8,192,128]{2,1,0:T(8,128)(2,1)} %shard_map.93), calls=%async_computation.1 | async-start | bytes 786432 | tf_op jit(solution)/shard_map/all_to_all | solution.py:378
  117.5 0.7 copy-start
  120.9 2.8 %copy-start.6 = (bf16[2,2,128,384]{3,2,1,0:T(8,128)(2,1)S(1)}, bf16[2,2,128,384]{3,2,1,0:T(8,128)(2,1)}, u32[]{:S(2)}) copy-start(bf16[2,2,128,384]{3,2,1,0:T(8,128)(2,1)} %copy-done.5) | copy-start | bytes 1179652
  143.6 7.3 %collective-permute-start.22 = (bf16[128,384]{1,0:T(8,128)(2,1)S(1)}, bf16[128,384]{1,0:T(8,128)(2,1)S(1)}, u32[]{:S(2)}, u32[]{:S(2)}) collective-permute-start(bf16[128,384]{1,0:T(8,128)(2,1)S(1)} %get-tuple-element.68), channel_id=1, source_target_pairs={{0,8},{8,0},{16,24},{24,16},{32,40},{40,32},{48,56},{56,48},{64,72... | collective-permute-start | bytes 294920 | tf_op jit(solution)/shard_map/ppermute | solution.py:329
  147.7 5.9 %collective-permute-start.23 = (bf16[128,384]{1,0:T(8,128)(2,1)S(1)}, bf16[128,384]{1,0:T(8,128)(2,1)S(1)}, u32[]{:S(2)}, u32[]{:S(2)}) collective-permute-start(bf16[128,384]{1,0:T(8,128)(2,1)S(1)} %get-tuple-element.69), channel_id=1, source_target_pairs={{0,128},{8,136},{16,144},{24,152},{32,160},{40,168},{48,176},{56,1... | collective-permute-start | bytes 294920 | tf_op jit(solution)/shard_map/ppermute | solution.py:329
  149.4 6.5 %collective-permute-start.24 = (bf16[128,384]{1,0:T(8,128)(2,1)S(1)}, bf16[128,384]{1,0:T(8,128)(2,1)S(1)}, u32[]{:S(2)}, u32[]{:S(2)}) collective-permute-start(bf16[128,384]{1,0:T(8,128)(2,1)S(1)} %get-tuple-element.70), channel_id=1, source_target_pairs={{0,136},{8,128},{16,152},{24,144},{32,168},{40,160},{48,184},{56,1... | collective-permute-start | bytes 294920 | tf_op jit(solution)/shard_map/ppermute | solution.py:329
